TPU v7x, 128 devices: a whole 4x4x4 slice. The times are simulated.
128 devices in a mesh: section: 16 (over y, x_hi, core), seq: 8 (over z, x_lo).
Axes of the slice: x: 4 (x_hi: 2, x_lo: 2; x = x_hi * 2 + x_lo), y: 4, z: 4, core: 2. Of those that a mesh axis runs over, the one named last changes fastest.
Arguments:
- section_input: bfloat16 [16, 1024, 2560], P('section', 'seq'), may hold values from -6 to 6
- state_in: float32 [16, 20, 128, 128], P('section'), may hold values from -24 to 24
- decay_table: float32 [16], replicated, may hold values from 0.96 to 1
- head_rate: int32 [16, 20], P('section'), may hold values from 0 to 15
- gates: float32 [16, 1024, 20], P('section', 'seq'), may hold values from 0.5 to 1
- query_gain: float32 [16, 2560], P('section'), may hold values from 0.25 to 1.75
- key_gain: float32 [16, 2560], P('section'), may hold values from 0.25 to 1.75
- out_gain: float32 [16, 2560], P('section'), may hold values from 0.25 to 1.75
- global_gain: float32 [2, 2560], replicated, may hold values from 0.25 to 1.75
- cache_kv: bfloat16 [8192, 5120], P(('section', 'seq')), may hold values from -480 to 480
- cache_pos: int32 [8192], P(('section', 'seq')), may hold values from 0 to 8191, each once
- span_start: int32 [16], P('section'), may hold values from 0 to 7168
Outputs:
- section_output: bfloat16 [16, 1024, 2560], P('section', 'seq')
- state_out: float32 [16, 20, 128, 128], P('section', None, 'seq')
- global_new: bfloat16 [8, 16, 8, 5120], P('seq', 'section')
All inputs are finite; a program needn't handle non-finite values.
Results may differ from a plain program's by a relative error of at most 0.014.
Values may be sent and summed in bfloat16 or wider, within the bound.
A program may use at most 384 MiB of HBM per device.

v0:
```python
import jax
import jax.numpy as jnp
from jax import lax
from jax.sharding import PartitionSpec as P

BLK = 128


EPSILON = 1e-06
MASKED_SCORE = -1e30
PRECISE = lax.Precision.HIGHEST


def prefix(part, axis, combine, identity):
    place = lax.axis_index(axis)
    gathered = jax.tree.map(lambda a: lax.all_gather(a, axis), part)
    state = jax.tree.map(lambda a, e: jnp.zeros_like(a) + jnp.asarray(e, a.dtype), part, identity)

    def one(hop, state):
        return combine(
            state, jax.tree.map(lambda a: lax.dynamic_index_in_dim(a, hop, 0, False), gathered)
        )

    return lax.fori_loop(0, place, one, state)


def passed_along(block, axis, distance):
    devices = range(lax.axis_size(axis))
    route = [((i - distance) % len(devices), i) for i in devices]
    return lax.ppermute(block, axis, route)


def from_root(value, axis, source):
    kept = jnp.where(lax.axis_index(axis) == source, value, 0).astype(value.dtype)
    return lax.psum(kept, axis)


def rms_rows(values):
    return values * lax.rsqrt(jnp.mean(values * values, axis=-1, keepdims=True) + EPSILON)


def block_terms(queries, key_rows, values, logdecay):
    block_len = queries.shape[0]
    cumulative = jnp.cumsum(logdecay, axis=0)
    ending = cumulative[-1]
    scores = jnp.einsum("thd,shd->hts", queries, key_rows, preferred_element_type=jnp.float32)
    causal = (jnp.arange(block_len)[:, None] >= jnp.arange(block_len)[None, :])[None]
    differences = cumulative.T[:, :, None] - cumulative.T[:, None, :]
    weights = jnp.where(causal, scores * jnp.exp(jnp.where(causal, differences, 0.0)), 0.0).astype(
        jnp.bfloat16
    )
    inside = jnp.einsum("hts,shd->thd", weights, values, preferred_element_type=jnp.float32)
    fading = jnp.exp(ending[None, :] - cumulative)
    update = jnp.einsum(
        "thd,the->hde",
        key_rows.astype(jnp.float32) * fading[:, :, None],
        values.astype(jnp.float32),
        precision=PRECISE,
    )
    return (inside, jnp.exp(cumulative), jnp.exp(ending), update)


def join_states(earlier, later):
    return (earlier[0] * later[0], later[0][:, None, None] * earlier[1] + later[1])


def local(
    section_input,
    state_in,
    decay_table,
    head_rate,
    gates,
    query_gain,
    key_gain,
    out_gain,
    global_gain,
    cache_kv,
    cache_pos,
    span_start,
):
    inputs = section_input[0]
    tok_rows, hidden_width = inputs.shape
    head_count = head_rate.shape[1]
    head_size = hidden_width // head_count
    sections = lax.axis_size("section")
    half_sections = sections // 2
    seq_count = lax.axis_size("seq")
    section_at = lax.axis_index("section")
    seq_at = lax.axis_index("seq")
    is_self = section_at < half_sections
    blocks = tok_rows // BLK
    row_count = head_size // seq_count
    normed = rms_rows(inputs.astype(jnp.float32))
    queries = (normed * query_gain[0]).astype(jnp.bfloat16)
    key_rows = (normed * key_gain[0]).astype(jnp.bfloat16)
    table_logs = jnp.log(decay_table)
    picked = jnp.sum(
        jnp.where(
            head_rate[0][:, None] == jnp.arange(table_logs.shape[0], dtype=jnp.int32)[None, :],
            table_logs[None, :],
            0.0,
        ),
        axis=1,
    )
    logdecay = picked[None, :] + jnp.log(gates[0])
    shaped_q = queries.reshape(blocks, BLK, head_count, head_size)
    shaped_k = key_rows.reshape(blocks, BLK, head_count, head_size)
    shaped_v = inputs.reshape(blocks, BLK, head_count, head_size)

    def local_blocks(unused):
        return jax.vmap(block_terms)(
            shaped_q, shaped_k, shaped_v, logdecay.reshape(blocks, BLK, head_count)
        )

    def skip_blocks(unused):
        return (
            jnp.zeros((blocks, BLK, head_count, head_size), jnp.float32),
            jnp.zeros((blocks, BLK, head_count), jnp.float32),
            jnp.zeros((blocks, head_count), jnp.float32),
            jnp.zeros((blocks, head_count, head_size, head_size), jnp.float32),
        )

    inside, growth, fading, update = lax.cond(is_self, local_blocks, skip_blocks, 0)
    total_fade = fading[0]
    total_update = update[0]
    start_state = state_in[0]
    identity = (jnp.ones_like(total_fade), jnp.zeros_like(total_update))
    before_fade, before_update = prefix((total_fade, total_update), "seq", join_states, identity)
    entering = before_fade[:, None, None] * start_state + before_update
    all_fades = lax.all_gather(total_fade[None], "seq", axis=0, tiled=True)
    later_fades = jnp.where(jnp.arange(seq_count)[:, None] > seq_at, all_fades, 1.0)
    suffix = jnp.prod(later_fades, axis=0)
    whole_fade = jnp.prod(all_fades, axis=0)
    summed = lax.psum_scatter(
        (suffix[:, None, None] * total_update).astype(jnp.bfloat16),
        "seq",
        scatter_dimension=1,
        tiled=True,
    ).astype(jnp.float32)
    state_rows = summed + lax.dynamic_slice_in_dim(
        whole_fade[:, None, None] * start_state, seq_at * row_count, row_count, 1
    )

    def self_mix(entered):
        carried_in = jnp.einsum(
            "thd,hde->the",
            shaped_q[0].astype(jnp.float32) * growth[0][:, :, None],
            entered,
            precision=PRECISE,
        )
        outputs = [inside[0] + carried_in]
        return rms_rows(jnp.concatenate(outputs, axis=0)).reshape(tok_rows, hidden_width)

    def no_mix(entered):
        return jnp.zeros((tok_rows, hidden_width), jnp.float32)

    selfmix = lax.cond(is_self, self_mix, no_mix, entering)
    kept_rows = lax.dynamic_slice_in_dim(start_state, seq_at * row_count, row_count, 1)
    state_local = jnp.where(is_self, state_rows, kept_rows)
    gathered_q = lax.all_gather(queries, "seq", axis=0, tiled=True)
    gathered_kv = lax.all_gather(cache_kv, "section", axis=0, tiled=True)
    gathered_pos = lax.all_gather(cache_pos, "section", axis=0, tiled=True)
    span_len = gathered_q.shape[0]
    places = span_start[0] + jnp.arange(span_len, dtype=jnp.int32)
    visible = gathered_pos[None, :] <= places[:, None]
    scale = head_size ** (-0.5)

    def attend_all(unused):

        def one_head(head_at):
            query_head = lax.dynamic_slice_in_dim(gathered_q, head_at * head_size, head_size, 1)
            key_head = lax.dynamic_slice_in_dim(gathered_kv, head_at * head_size, head_size, 1)
            value_head = lax.dynamic_slice_in_dim(
                gathered_kv, hidden_width + head_at * head_size, head_size, 1
            )
            scores = (
                jnp.einsum("qd,kd->qk", query_head, key_head, preferred_element_type=jnp.float32)
                * scale
            )
            scores = jnp.where(visible, scores, MASKED_SCORE)
            highest = jnp.max(scores, axis=1)
            likely = jnp.exp(scores - highest[:, None])
            totals = jnp.sum(likely, axis=1)
            pieces = jnp.dot(
                likely.astype(jnp.bfloat16), value_head, preferred_element_type=jnp.float32
            )
            return (highest, totals, pieces)

        return lax.map(one_head, jnp.arange(head_count, dtype=jnp.int32))

    def no_attend(unused):
        return (
            jnp.zeros((head_count, span_len), jnp.float32),
            jnp.ones((head_count, span_len), jnp.float32),
            jnp.zeros((head_count, span_len, head_size), jnp.float32),
        )

    highest, totals, pieces = lax.cond(is_self, no_attend, attend_all, 0)
    got_high, got_totals, got_pieces = (
        lax.all_to_all(highest[None], "seq", split_axis=2, concat_axis=0, tiled=True),
        lax.all_to_all(totals[None], "seq", split_axis=2, concat_axis=0, tiled=True),
        lax.all_to_all(pieces[None], "seq", split_axis=2, concat_axis=0, tiled=True),
    )
    overall = jnp.max(got_high, axis=0)
    factor = jnp.exp(got_high - overall[None])
    attended = (
        jnp.sum(got_pieces * factor[..., None], axis=0)
        / jnp.sum(got_totals * factor, axis=0)[..., None]
    )
    attended_rows = jnp.transpose(attended, (1, 0, 2)).reshape(tok_rows, hidden_width)
    mixed = jnp.where(is_self, selfmix, attended_rows)
    result = (inputs.astype(jnp.float32) + mixed * out_gain[0]).astype(jnp.bfloat16)
    section_output = passed_along(result, "section", 1)
    source = half_sections - 1
    per_section = tok_rows // sections
    nfresh = rms_rows(result.astype(jnp.float32))
    projected = jnp.concatenate([nfresh * global_gain[0], nfresh * global_gain[1]], axis=1).astype(
        jnp.bfloat16
    )
    arrived = from_root(projected, "section", source)
    fresh_rows = lax.dynamic_slice_in_dim(arrived, section_at * per_section, per_section, 0)
    return (section_output[None], state_local[None], fresh_rows[None, None])


def solution(mesh):
    return jax.shard_map(
        local,
        mesh=mesh,
        in_specs=(
            P("section", "seq", None),
            P("section", None, None, None),
            P(),
            P("section", None),
            P("section", "seq", None),
            P("section", None),
            P("section", None),
            P("section", None),
            P(),
            P(("section", "seq"), None),
            P(("section", "seq")),
            P("section"),
        ),
        out_specs=(
            P("section", "seq", None),
            P("section", None, "seq", None),
            P("seq", "section", None, None),
        ),
        check_vma=False,
    )
```

profile of v0, /device:TPU:17, one launch (start us, length us, event | category | flops | bytes accessed | tf_op | source)
XLA Modules:
  0.0 789.7 jit_solution(645206208575823135)
XLA Ops:
  11.2 1.7 multiply_convert_fusion.1
  13.0 1.5 conditional.3
  16.7 16.6 %all-reduce = s32[1024]{0:T(1024)S(1)} all-reduce(s32[1024]{0:T(1024)S(1)} %dynamic-update-slice), channel_id=1, replica_groups=mesh['section'=16,'seq'=8] {'section'}, use_global_device_ids=true, to_apply=%add | all-reduce | flops 1024 | bytes 8192
  33.3 88.5 %all-gather.7.cloned.1.call-done = bf16[1024,2560]{0,1:T(8,128)(2,1)} async-done(((bf16[128,2560]{0,1:T(8,128)(2,1)}), bf16[1024,2560]{0,1:T(8,128)(2,1)}) %all-gather.7.cloned.1.call-update) | async-done | bytes 5242896 | tf_op jit(solution)/shard_map/all_gather | solution.py:160
  121.8 84.1 %all-gather.9.cloned.1.call-done = bf16[1024,5120]{1,0:T(8,128)(2,1)} async-done(((bf16[64,5120]{1,0:T(8,128)(2,1)}), bf16[1024,5120]{1,0:T(8,128)(2,1)}) %all-gather.9.cloned.1.call-update) | async-done | bytes 10485776 | tf_op jit(solution)/shard_map/all_gather | solution.py:161
  205.9 239.0 %conditional.5 = (f32[20,1024]{1,0:T(8,128)S(1)}, f32[20,1024]{1,0:T(8,128)}, f32[20,1024,128]{2,1,0:T(8,128)}) conditional(s32[]{:T(128)} %convert_element_type.84, (s32[1024]{0:T(1024)S(1)}, s32[1]{0:T(128)}, s32[1024,1]{0,1:T(1,128)S(1)}, bf16[1024,2560]{0,1:T(8,128)(2,1)}, bf16[1024,5120]{1,0:T(8,128)(2,1)}) %tuple.53, () %tuple.54), branch_computations={%region_10.15_spmd, %region_15.16_spmd} | conditional | flops 551549952 | bytes 30737436 | solution.py:198
  206.5 238.3 %while.28 = (s32[]{:T(128)}, f32[20,1024]{1,0:T(8,128)S(1)}, f32[20,1024]{1,0:T(8,128)}, f32[20,1024,128]{2,1,0:T(8,128)}, s32[20]{0:T(128)S(1)}, /*index=5*/bf1...) while((s32[]{:T(128)}, f32[20,1024]{1,0:T(8,128)S(1)}, ...), condition=%wide.region_14.14_spmd.clone, body=%wide.region_11.13_spmd.clone.sunk | while | flops 551548928 | bytes 30729008 | solution.py:189
  207.8 3.7 fusion.71
  211.6 4.4 fusion.73
  219.7 3.7 fusion.71
  223.4 4.4 fusion.73
  231.7 3.8 fusion.71
  235.4 4.4 fusion.73
  243.6 3.7 fusion.71
  247.3 4.4 fusion.73
  255.5 3.7 fusion.71
  259.2 4.4 fusion.73
  267.4 3.7 fusion.71
  271.2 4.4 fusion.73
  279.3 3.7 fusion.71
  283.1 4.3 fusion.73
  291.2 3.7 fusion.71
  295.0 4.4 fusion.73
  303.2 3.7 fusion.71
  306.9 4.4 fusion.73
  315.1 3.7 fusion.71
  318.9 4.4 fusion.73
  327.1 3.7 fusion.71
  330.8 4.4 fusion.73
  339.0 3.7 fusion.71
  342.7 4.4 fusion.73
  350.9 3.8 fusion.71
  354.6 4.4 fusion.73
  362.8 3.7 fusion.71
  366.6 4.4 fusion.73
  374.7 3.7 fusion.71
  378.5 4.4 fusion.73
  386.7 3.7 fusion.71
  390.4 4.4 fusion.73
  398.6 3.7 fusion.71
  402.3 4.4 fusion.73
  410.5 3.7 fusion.71
  414.2 4.4 fusion.73
  422.4 3.7 fusion.71
  426.1 4.3 fusion.73
  434.3 3.7 fusion.71
  438.0 4.4 fusion.73
  445.7 2.0 reduce.12
  448.8 4.1 all-to-all-start.1
  453.1 2.0 reduce.10
  456.2 2.0 all-to-all-done.1
  458.2 3.4 all-to-all-start.2
  461.6 13.4 %copy.155 = f32[1,20,1024,128]{3,0,1,2:T(1,128)} copy(f32[1,20,1024,128]{3,2,1,0:T(8,128)} %bitcast.128) | data formatting | bytes 20971520 | tf_op jit(solution)/shard_map/broadcast_in_dim | solution.py:202
  475.0 5.1 all-to-all-start
  480.3 122.1 %all-gather = f32[8,1,20]{2,1,0:T(1,128)S(1)} all-gather(f32[1,1,20]{2,1,0:T(1,128)S(1)} %bitcast.153), channel_id=1, replica_groups=mesh['section'=16,'seq'=8] {'seq'}, dimensions={0}, use_global_device_ids=true | all-gather | bytes 720 | tf_op jit(solution)/shard_map/all_gather | solution.py:16
  609.6 5.2 copy.156
  614.8 3.2 multiply_reduce_fusion.1
  619.4 1.8 copy.162
  626.3 6.8 collective-permute-start
  633.1 6.7 reduce-scatter.2.cloned.1.call-done
  639.8 1.8 fusion.58
  641.6 1.6 collective-permute-done
  644.3 136.1 %all-reduce.3.cloned.1.call-done = bf16[128,5120]{0,1:T(8,128)(2,1)} async-done(((bf16[128,5120]{0,1:T(8,128)(2,1)}), bf16[128,5120]{0,1:T(8,128)(2,1)}) %all-reduce.3.cloned.1.call-update) | async-done | bytes 1310736 | tf_op jit(solution)/shard_map/psum | solution.py:35
  780.4 1.7 constant_dynamic-slice_fusion
  (217 shorter events, 88.3 us)
Async XLA Ops:
  7.2 1.8 copy-start.10
  7.2 114.6 %all-gather.7.cloned.1.call-start = ((), (), s32[]{:S(2)}) async-start(), calls=%async_computation.5 | async-start | bytes 5898240 | tf_op jit(solution)/shard_map/all_gather | solution.py:160
  9.0 2.1 copy-start.11
  10.3 2.6 copy-start.9
  10.4 2.6 copy-start.13
  10.4 2.6 copy-start.14
  10.4 195.5 %all-gather.9.cloned.1.call-start = ((), (), s32[]{:S(2)}) async-start(), calls=%async_computation.6 | async-start | bytes 11141120 | tf_op jit(solution)/shard_map/all_gather | solution.py:161
  11.1 592.6 %all-gather.5.cloned.1.call-start = ((), (), s32[]{:S(2)}) async-start(), calls=%async_computation.4 | async-start | bytes 11796480 | tf_op jit(solution)/shard_map/all_gather | solution.py:16
  14.5 191.4 %copy-start.4 = (f32[1,128,20,128]{3,1,2,0:T(8,128)}, f32[1,128,20,128]{3,1,2,0:T(8,128)S(1)}, u32[]{:S(2)}) copy-start(f32[1,128,20,128]{3,1,2,0:T(8,128)S(1)} %get-tuple-element.230) | copy-start | bytes 3932164
  14.5 0.7 copy-start.16
  14.5 1.9 copy-start.15
  211.6 4.4 copy-start
  223.4 4.5 copy-start
  235.4 4.4 copy-start
  247.3 4.4 copy-start
  259.2 4.4 copy-start
  271.2 4.4 copy-start
  283.1 4.4 copy-start
  295.0 4.4 copy-start
  306.9 4.4 copy-start
  318.9 4.4 copy-start
  330.8 4.4 copy-start
  342.7 4.4 copy-start
  354.6 4.4 copy-start
  366.6 4.4 copy-start
  378.5 4.4 copy-start
  390.4 4.4 copy-start
  402.3 4.4 copy-start
  414.2 4.4 copy-start
  426.1 4.3 copy-start
  438.0 4.4 copy-start
  444.9 8.0 %copy-start.7 = (f32[20,1024]{1,0:T(8,128)S(1)}, f32[20,1024]{1,0:T(8,128)}, u32[]{:S(2)}) copy-start(f32[20,1024]{1,0:T(8,128)} %get-tuple-element.238) | copy-start | bytes 245764
  448.8 9.4 %all-to-all-start.1 = ((f32[8,1,2560]{2,1,0:T(1,128)}), f32[8,1,2560]{2,1,0:T(1,128)S(1)}, u32[]{:S(2)}, u32[]{:S(2)}) async-start(f32[8,1,2560]{2,1,0:T(1,128)} %reshape.232), calls=%async_computation.1 | async-start | bytes 163840 | tf_op jit(solution)/shard_map/all_to_all | solution.py:200
  458.2 16.8 %all-to-all-start.2 = ((f32[8,1,2560]{2,1,0:T(1,128)}), f32[8,1,2560]{2,1,0:T(1,128)S(1)}, u32[]{:S(2)}, u32[]{:S(2)}) async-start(f32[8,1,2560]{2,1,0:T(1,128)} %reshape.234), calls=%async_computation.2 | async-start | bytes 163840 | tf_op jit(solution)/shard_map/all_to_all | solution.py:201
  475.0 134.6 %all-to-all-start = ((f32[1,20,1024,128]{3,0,1,2:T(1,128)}), f32[1,20,1024,128]{3,0,1,2:T(1,128)}, u32[]{:S(2)}, u32[]{:S(2)}) async-start(f32[1,20,1024,128]{3,0,1,2:T(1,128)} %copy.155), calls=%async_computation | async-start | bytes 20971520 | tf_op jit(solution)/shard_map/all_to_all | solution.py:202
  480.2 159.6 %reduce-scatter.2.cloned.1.call-start = ((), (), s32[]{:S(2)}) async-start(), calls=%async_computation.7 | async-start | bytes 737280 | tf_op jit(solution)/shard_map/reduce_scatter | solution.py:134
  602.5 1.1 copy-start.12
  602.5 1.1 copy-start.8
  603.5 176.9 %all-reduce.3.cloned.1.call-start = ((), (), s32[]{:S(2)}) async-start(), calls=%async_computation.8 | async-start | bytes 2621440 | tf_op jit(solution)/shard_map/psum | solution.py:35
  603.9 1.1 copy-start.1
  605.3 4.2 copy-start.2
  619.4 1.8 copy-start.3
  621.7 0.8 copy-start.5
  625.2 1.1 copy-start.6
  626.3 16.9 %collective-permute-start = (bf16[128,2560]{0,1:T(8,128)(2,1)S(1)}, bf16[128,2560]{0,1:T(8,128)(2,1)S(1)}, u32[]{:S(2)}, u32[]{:S(2)}) collective-permute-start(bf16[128,2560]{0,1:T(8,128)(2,1)S(1)} %copy-done.6), channel_id=1, source_target_pairs={{120,0},{0,8},{8,16},{16,24},{24,32},{32,40},{40,48},{48,56},{56,6... | collective-permute-start | bytes 1966088 | tf_op jit(solution)/shard_map/ppermute | solution.py:30
Sparse Core Ops, SparseCore 0:
  10.5 111.2 all-gather.6
  124.2 81.5 all-gather.8
  207.5 206.6 all-gather.4
  603.6 36.1 reduce-scatter.1
  642.1 138.2 all-reduce.2
where the time goes:
time: 801 us; the launch traced here: 790 us
  waiting for transfers between devices  320 us (40%)
  matrix products  163 us (20%)
  blocking collectives  139 us (17%)
  local copies, waits for them, and re-layouts  78.7 us (10%)
  other arithmetic  41.1 us (5%)
  starting transfers between devices  19.5 us (2%)
  between operations  14.9 us (2%)
  loops' own time  14.3 us (2%)
    psum x1, waiting for transfers between devices, from_root(): return lax.psum(kept, axis)  136 us
    all_gather x1, blocking collectives, prefix(): gathered = jax.tree.map(lambda a: lax.all_gather(a, axis), part)  122 us
    all_gather x1, waiting for transfers between devices, local(): gathered_q = lax.all_gather(queries, 'seq', axis=0, tiled=True)  88.5 us
    dot_general x20, matrix products, one_head(): jnp.dot(likely.astype(jnp.bfloat16), value_head, preferred_element_type=j...  87.8 us
    all_gather x1, waiting for transfers between devices, local(): gathered_kv = lax.all_gather(cache_kv, 'section', axis=0, tiled=True)  84.1 us
    dot_general x20, matrix products, one_head(): jnp.einsum('qd,kd->qk', query_head, key_head, preferred_element_type=jnp....  74.8 us
    dynamic_update_slice x40, local copies, waits for them, and re-layouts, attend_all(): return lax.map(one_head, jnp.arange(head_count, dtype=jnp.int32))  29.3 us
    reduce_sum x20, other arithmetic, one_head(): totals = jnp.sum(likely, axis=1)  20.5 us
  transfers between devices with their start and end apart: 9, of which 6 were waited for; matrix products, arithmetic and copies ran while one was open for 35% of the time, Pallas kernels for 0%

commit v1 on v0

v1 whole, which is shorter than its diff:
```python
import functools

import jax
import jax.numpy as jnp
from jax import lax
from jax.experimental import pallas as pl
from jax.experimental.pallas import tpu as pltpu
from jax.sharding import PartitionSpec as P

MESH = pl.DeviceIdType.MESH
EPSILON = 1e-06
MASKED_SCORE = -1e30
LOG2E = 1.4426950408889634
HD = 2560
HEADS = 20
HDIM = 128
GROUP = 640
HALF = 64
KEYS = 2048


def place_of():
    section = lax.axis_index("section")
    seq = lax.axis_index("seq")
    return section // 4, ((section // 2) % 2) * 2 + seq % 2, seq // 2, section % 2


def device_at(y, x, z, core):
    return (y * 4 + (x // 2) * 2 + core, z * 2 + x % 2)


def shifted(value, by):
    return lax.rem(value + by + 4, 4)


def greet(peers):
    barrier = pltpu.get_barrier_semaphore()
    for peer in peers:
        pl.semaphore_signal(barrier, inc=1, device_id=peer, device_id_type=MESH)
    pl.semaphore_wait(barrier, len(peers))


def remote(src, dst, send_sem, recv_sem, peer):
    return pltpu.make_async_remote_copy(
        src_ref=src,
        dst_ref=dst,
        send_sem=send_sem,
        recv_sem=recv_sem,
        device_id=peer,
        device_id_type=MESH,
    )


NEAR_Y = [(dy, dx) for dy in (0, 1, 3, 2) for dx in (0, 1, 3, 2)]
NEAR_Z = [(dz, dx) for dz in (0, 1, 3, 2) for dx in (0, 1, 3, 2)]


def exchange_kernel(
    x_ref,
    gain_ref,
    kv_ref,
    meta_ref,
    update_ref,
    fade_ref,
    k_out,
    v_out,
    meta_out,
    q_out,
    at_x,
    at_gain,
    update_out,
    fade_out,
    queries,
    half_send,
    half_recv,
    gain_send,
    gain_recv,
    kv_send,
    kv_recv,
    fwd_send,
    fwd_recv,
    q_send,
    q_recv,
    u_send,
    u_recv,
    local_sem,
):
    y, x, z, core = place_of()
    is_self = y < 2
    sibling = device_at(y, x, z, 1 - core)
    partner = device_at(3 - y, x, z, core)
    peers = [device_at(shifted(y, dy), shifted(x, dx), z, core) for dy, dx in NEAR_Y[1:]]
    peers += [device_at(y, shifted(x, dx), shifted(z, dz), core) for dz, dx in NEAR_Z[4:]]
    peers.append(sibling)
    greet(peers)

    half_copy = remote(x_ref.at[pl.ds(HALF, HALF)], at_x, half_send, half_recv, partner)
    gain_copy = remote(gain_ref, at_gain, gain_send, gain_recv, partner)

    @pl.when(jnp.logical_not(is_self))
    def _():
        half_copy.start()
        gain_copy.start()

    slot = pl.ds(pl.multiple_of((x * 4 + y) * 128 + core * 64, 64), 64)
    meta_slot = (x * 4 + y) * 2 + core

    def kv_pieces(column_place):
        k_cols = pl.ds(pl.multiple_of(column_place * GROUP, 128), GROUP)
        v_cols = pl.ds(pl.multiple_of(HD + column_place * GROUP, 128), GROUP)
        return (
            (meta_ref, meta_out.at[meta_slot]),
            (kv_ref.at[:, k_cols], k_out.at[slot]),
            (kv_ref.at[:, v_cols], v_out.at[slot]),
        )

    kv_copies = []
    for at, (dy, dx) in enumerate(NEAR_Y):
        if at == 0:
            continue
        to_x = shifted(x, dx)
        peer = device_at(shifted(y, dy), to_x, z, core)
        for kind, (src, dst) in enumerate(kv_pieces(to_x)):
            copy = remote(src, dst, kv_send.at[at, kind], kv_recv.at[at, kind], peer)
            copy.start()
            kv_copies.append(copy)
    own_copies = []
    fwd_copies = []
    for kind, (src, dst) in enumerate(kv_pieces(x)):
        copy = pltpu.make_async_copy(src, dst, local_sem.at[kind])
        copy.start()
        own_copies.append(copy)
        copy = remote(src, dst, fwd_send.at[0, kind], fwd_recv.at[0, kind], sibling)
        copy.start()
        fwd_copies.append(copy)

    seq = z * 2 + x % 2
    u_copies = []
    for at in range(8):
        dz, flip = at // 2, at % 2
        to_z, to_x = shifted(z, dz), (x // 2) * 2 + lax.rem(x + flip, 2)
        to_seq = to_z * 2 + to_x % 2
        rows = pl.ds(pl.multiple_of(to_seq * 16, 16), 16)
        pairs = ((update_ref.at[:, rows, :], update_out.at[seq]), (fade_ref, fade_out.at[seq]))
        for kind, (src, dst) in enumerate(pairs):
            if at == 0:
                copy = pltpu.make_async_copy(src, dst, local_sem.at[3 + kind])
            else:
                copy = remote(
                    src, dst, u_send.at[at, kind], u_recv.at[at, kind], device_at(y, to_x, to_z, core)
                )
            u_copies.append(copy)

    @pl.when(is_self)
    def _():
        for copy in u_copies:
            copy.start()
        half_copy.wait_recv()
        gain_copy.wait_recv()

    @pl.when(jnp.logical_not(is_self))
    def _():
        at_x[...] = x_ref[0:HALF, :]
        at_gain[...] = gain_ref[...]

    rows = at_x[...].astype(jnp.float32)
    normed = rows * lax.rsqrt(jnp.mean(rows * rows, axis=1, keepdims=True) + EPSILON)
    queries[...] = (normed * at_gain[0:1, :]).astype(jnp.bfloat16)

    q_copies = []
    q_slot = pl.ds(pl.multiple_of((z * 4 + x) * HALF, HALF), HALF)
    for at, (dz, dx) in enumerate(NEAR_Z):
        to_x, to_z = shifted(x, dx), shifted(z, dz)
        src = queries.at[:, pl.ds(pl.multiple_of(to_x * GROUP, 128), GROUP)]
        dst = q_out.at[q_slot]
        if at == 0:
            copy = pltpu.make_async_copy(src, dst, local_sem.at[5])
        else:
            copy = remote(src, dst, q_send.at[at], q_recv.at[at], device_at(y, to_x, to_z, core))
        copy.start()
        q_copies.append(copy)

    def came_from(at):
        dy, dx = NEAR_Y[at]
        from_x, from_y = shifted(x, -dx), shifted(y, -dy)
        here = pl.ds(pl.multiple_of((from_x * 4 + from_y) * 128 + core * 64, 64), 64)
        meta_here = (from_x * 4 + from_y) * 2 + core
        return (meta_out.at[meta_here], k_out.at[here], v_out.at[here])

    for at in range(1, 16):
        for kind, ref in enumerate(came_from(at)):
            remote(ref, ref, kv_send.at[at, kind], kv_recv.at[at, kind], sibling).wait_recv()
            copy = remote(ref, ref, fwd_send.at[at, kind], fwd_recv.at[at, kind], sibling)
            copy.start()
            fwd_copies.append(copy)

    for copy in own_copies:
        copy.wait()
    for copy in fwd_copies:
        copy.wait()
    for copy in kv_copies:
        copy.wait_send()
    for copy in q_copies:
        copy.wait()

    @pl.when(is_self)
    def _():
        for copy in u_copies:
            copy.wait()

    @pl.when(jnp.logical_not(is_self))
    def _():
        half_copy.wait_send()
        gain_copy.wait_send()


def exchange(x, gains, kv, meta, update, fade):
    any_spec = pl.BlockSpec(memory_space=pl.ANY)
    vmem = pl.BlockSpec(memory_space=pltpu.VMEM)
    dma = pltpu.SemaphoreType.DMA
    return pl.pallas_call(
        exchange_kernel,
        out_shape=(
            jax.ShapeDtypeStruct((KEYS, GROUP), jnp.bfloat16),
            jax.ShapeDtypeStruct((KEYS, GROUP), jnp.bfloat16),
            jax.ShapeDtypeStruct((32, 8, 128), jnp.int32),
            jax.ShapeDtypeStruct((1024, GROUP), jnp.bfloat16),
            jax.ShapeDtypeStruct((HALF, HD), jnp.bfloat16),
            jax.ShapeDtypeStruct((8, HD), jnp.float32),
            jax.ShapeDtypeStruct((8, HEADS, 16, HDIM), jnp.bfloat16),
            jax.ShapeDtypeStruct((8, 8, 128), jnp.float32),
        ),
        in_specs=[vmem, vmem, any_spec, any_spec, any_spec, any_spec],
        out_specs=(any_spec, any_spec, any_spec, any_spec, vmem, vmem, any_spec, any_spec),
        scratch_shapes=[
            pltpu.VMEM((HALF, HD), jnp.bfloat16),
            dma,
            dma,
            dma,
            dma,
            dma((16, 3)),
            dma((16, 3)),
            dma((16, 3)),
            dma((16, 3)),
            dma((16,)),
            dma((16,)),
            dma((8, 2)),
            dma((8, 2)),
            dma((8,)),
        ],
        compiler_params=pltpu.CompilerParams(
            collective_id=0, has_side_effects=True, vmem_limit_bytes=32 * 1024 * 1024
        ),
        name="exchange",
    )(x, gains, kv, meta, update, fade)


QBLOCK = 256


def attend_kernel(starts, pos_ref, q_ref, k_ref, v_ref, o_ref, lse_ref):
    head = pl.program_id(1)
    block = pl.program_id(0)
    index = lax.broadcasted_iota(jnp.int32, (QBLOCK, 1), 0)
    x = index // HALF
    token = block * 256 + (x % 2) * 128 + starts[2] * HALF + index % HALF
    places = jnp.where(x < 2, starts[0], starts[1]) + token
    scores = lax.dot_general(
        q_ref[...], k_ref[...], (((1,), (1,)), ((), ())), preferred_element_type=jnp.float32
    )
    scores = jnp.where(pos_ref[...] <= places, scores, MASKED_SCORE)
    highest = jnp.max(scores, axis=1, keepdims=True)
    factor = HDIM ** (-0.5) * LOG2E
    likely = jnp.exp2((scores - highest) * factor)
    totals = jnp.sum(likely, axis=1, keepdims=True)
    pieces = jnp.dot(likely.astype(jnp.bfloat16), v_ref[...], preferred_element_type=jnp.float32)
    o_ref[...] = (pieces / totals).astype(jnp.bfloat16)
    lse = highest * (HDIM ** (-0.5)) + jnp.log(totals)
    lane = lax.broadcasted_iota(jnp.int32, (QBLOCK, 128), 1)

    @pl.when(head == 0)
    def _():
        lse_ref[...] = jnp.broadcast_to(lse, (QBLOCK, 128))

    @pl.when(head > 0)
    def _():
        lse_ref[...] = jnp.where(lane == head, lse, lse_ref[...])


def attend(starts, pos, q, k, v):
    return pl.pallas_call(
        attend_kernel,
        out_shape=(
            jax.ShapeDtypeStruct((1024, GROUP), jnp.bfloat16),
            jax.ShapeDtypeStruct((1024, 128), jnp.float32),
        ),
        grid=(1024 // QBLOCK, 5),
        in_specs=[
            pl.BlockSpec(memory_space=pltpu.SMEM),
            pl.BlockSpec((1, KEYS), lambda i, h: (0, 0)),
            pl.BlockSpec((QBLOCK, HDIM), lambda i, h: (i, h)),
            pl.BlockSpec((KEYS, HDIM), lambda i, h: (0, h)),
            pl.BlockSpec((KEYS, HDIM), lambda i, h: (0, h)),
        ],
        out_specs=(
            pl.BlockSpec((QBLOCK, HDIM), lambda i, h: (i, h)),
            pl.BlockSpec((QBLOCK, 128), lambda i, h: (i, 0)),
        ),
        compiler_params=pltpu.CompilerParams(vmem_limit_bytes=32 * 1024 * 1024),
        cost_estimate=pl.CostEstimate(
            flops=4 * 1024 * KEYS * GROUP, bytes_accessed=10_000_000, transcendentals=1024 * KEYS * 5
        ),
        name="attend",
    )(starts, pos, q, k, v)


def returning_kernel(
    o_ref, lse_ref, enter_ref, o_out, lse_out, enter_out, o_send, o_recv, e_send, e_recv, local_sem
):
    y, x, z, core = place_of()
    is_self = y < 2
    greet([device_at(y, shifted(x, dx), shifted(z, dz), core) for dz, dx in NEAR_Z[1:]])
    copies = []
    columns = pl.ds(pl.multiple_of(x * GROUP, 128), GROUP)
    for at, (dz, dx) in enumerate(NEAR_Z):
        to_x, to_z = shifted(x, dx), shifted(z, dz)
        rows = pl.ds(pl.multiple_of((to_z * 4 + to_x) * HALF, HALF), HALF)
        pairs = (
            (lse_ref.at[rows], lse_out.at[z, x]),
            (o_ref.at[rows], o_out.at[z, :, columns]),
        )
        for kind, (src, dst) in enumerate(pairs):
            if at == 0:
                copy = pltpu.make_async_copy(src, dst, local_sem.at[kind])
            else:
                copy = remote(
                    src, dst, o_send.at[at, kind], o_recv.at[at, kind], device_at(y, to_x, to_z, core)
                )
            copy.start()
            copies.append(copy)
    seq = z * 2 + x % 2
    e_copies = []
    for at in range(8):
        dz, flip = at // 2, at % 2
        to_z, to_x = shifted(z, dz), (x // 2) * 2 + lax.rem(x + flip, 2)
        src = enter_ref.at[to_z * 2 + to_x % 2]
        dst = enter_out.at[:, pl.ds(pl.multiple_of(seq * 16, 16), 16), :]
        if at == 0:
            copy = pltpu.make_async_copy(src, dst, local_sem.at[2])
        else:
            copy = remote(src, dst, e_send.at[at], e_recv.at[at], device_at(y, to_x, to_z, core))
        e_copies.append(copy)

    @pl.when(is_self)
    def _():
        for copy in e_copies:
            copy.start()

    for copy in copies:
        copy.wait()

    @pl.when(is_self)
    def _():
        for copy in e_copies:
            copy.wait()


def returning(o, lse, enter):
    any_spec = pl.BlockSpec(memory_space=pl.ANY)
    dma = pltpu.SemaphoreType.DMA
    return pl.pallas_call(
        returning_kernel,
        out_shape=(
            jax.ShapeDtypeStruct((4, HALF, HD), jnp.bfloat16),
            jax.ShapeDtypeStruct((4, 4, HALF, 128), jnp.float32),
            jax.ShapeDtypeStruct((HEADS, HDIM, HDIM), jnp.bfloat16),
        ),
        in_specs=[any_spec] * 3,
        out_specs=(any_spec,) * 3,
        scratch_shapes=[dma((16, 2)), dma((16, 2)), dma((8,)), dma((8,)), dma((3,))],
        compiler_params=pltpu.CompilerParams(collective_id=1, has_side_effects=True),
        name="returning",
    )(o, lse, enter)


def onward_kernel(att_ref, mix_ref, out_ref, fresh_ref, s_send, s_recv, f_send, f_recv, local_sem):
    section = lax.axis_index("section")
    seq = lax.axis_index("seq")
    greet([(lax.rem(section + by, 16), seq) for by in range(1, 16)])
    is_self = section < 8
    after = lax.rem(section + 1, 16)
    whole = remote(mix_ref, out_ref, s_send.at[0], s_recv.at[0], (after, seq))
    first = remote(att_ref, out_ref.at[pl.ds(0, HALF)], s_send.at[1], s_recv.at[1], (after, seq))
    helped = jnp.where(section < 4, section + 12, section + 4)
    target = lax.rem(helped + 1, 16)
    second = remote(att_ref, out_ref.at[pl.ds(HALF, HALF)], s_send.at[2], s_recv.at[2], (target, seq))

    def fresh_rows(to):
        return mix_ref.at[pl.ds(pl.multiple_of((to // 2) * 16, 16), 16)]

    own = pltpu.make_async_copy(fresh_rows(section), fresh_ref, local_sem)

    def fresh_copy(by):
        to = lax.rem(section + by, 16)
        return remote(fresh_rows(to), fresh_ref, f_send.at[by], f_recv, (to, seq))

    is_root = section == 7

    @pl.when(is_self)
    def _():
        whole.start()
        second.start()

    @pl.when(jnp.logical_not(is_self))
    def _():
        first.start()

    @pl.when(is_root)
    def _():
        own.start()
        for by in range(1, 16):
            fresh_copy(by).start()

    from_self = jnp.logical_and(section >= 1, section <= 8)

    @pl.when(from_self)
    def _():
        whole.wait_recv()

    @pl.when(jnp.logical_not(from_self))
    def _():
        first.wait_recv()
        second.wait_recv()

    @pl.when(is_self)
    def _():
        whole.wait_send()
        second.wait_send()

    @pl.when(jnp.logical_not(is_self))
    def _():
        first.wait_send()

    @pl.when(is_root)
    def _():
        own.wait()
        for by in range(1, 16):
            fresh_copy(by).wait_send()

    @pl.when(jnp.logical_not(is_root))
    def _():
        fresh_copy(1).wait_recv()


def onward(att, mix):
    any_spec = pl.BlockSpec(memory_space=pl.ANY)
    dma = pltpu.SemaphoreType.DMA
    return pl.pallas_call(
        onward_kernel,
        out_shape=(
            jax.ShapeDtypeStruct((128, HD), jnp.bfloat16),
            jax.ShapeDtypeStruct((16, HD), jnp.bfloat16),
        ),
        in_specs=[any_spec] * 2,
        out_specs=(any_spec,) * 2,
        scratch_shapes=[dma((3,)), dma((3,)), dma((16,)), dma, dma],
        compiler_params=pltpu.CompilerParams(collective_id=2, has_side_effects=True),
        name="onward",
    )(att, mix)


def rms_rows(values):
    return values * lax.rsqrt(jnp.mean(values * values, axis=-1, keepdims=True) + EPSILON)


def block_terms(queries, key_rows, values, logdecay):
    block_len = queries.shape[0]
    cumulative = jnp.cumsum(logdecay, axis=0)
    ending = cumulative[-1]
    scores = jnp.einsum("thd,shd->hts", queries, key_rows, preferred_element_type=jnp.float32)
    causal = (jnp.arange(block_len)[:, None] >= jnp.arange(block_len)[None, :])[None]
    differences = cumulative.T[:, :, None] - cumulative.T[:, None, :]
    weights = jnp.where(causal, scores * jnp.exp(jnp.where(causal, differences, 0.0)), 0.0).astype(
        jnp.bfloat16
    )
    inside = jnp.einsum("hts,shd->thd", weights, values, preferred_element_type=jnp.float32)
    fading = jnp.exp(ending[None, :] - cumulative)
    update = jnp.einsum(
        "thd,the->hde",
        (key_rows.astype(jnp.float32) * fading[:, :, None]).astype(jnp.bfloat16),
        values,
        preferred_element_type=jnp.float32,
    ).astype(jnp.bfloat16)
    return (inside, jnp.exp(cumulative), jnp.exp(ending), update)


def local(
    section_input,
    state_in,
    decay_table,
    head_rate,
    gates,
    query_gain,
    key_gain,
    out_gain,
    global_gain,
    cache_kv,
    cache_pos,
    span_start,
):
    inputs = section_input[0]
    section_at = lax.axis_index("section")
    seq_at = lax.axis_index("seq")
    is_self = section_at < 8
    y, _, z, core = place_of()

    table_logs = jnp.log(decay_table)
    picked = jnp.sum(
        jnp.where(
            head_rate[0][:, None] == jnp.arange(16, dtype=jnp.int32)[None, :],
            table_logs[None, :],
            0.0,
        ),
        axis=1,
    )

    def local_blocks(unused):
        normed = rms_rows(inputs.astype(jnp.float32))
        queries = (normed * query_gain[0]).astype(jnp.bfloat16)
        key_rows = (normed * key_gain[0]).astype(jnp.bfloat16)
        logdecay = picked[None, :] + jnp.log(gates[0])
        shape = (128, HEADS, HDIM)
        terms = block_terms(
            queries.reshape(shape), key_rows.reshape(shape), inputs.reshape(shape), logdecay
        )
        return (queries.reshape(shape),) + terms

    def skip_blocks(unused):
        return (
            jnp.zeros((128, HEADS, HDIM), jnp.bfloat16),
            jnp.zeros((128, HEADS, HDIM), jnp.float32),
            jnp.zeros((128, HEADS), jnp.float32),
            jnp.zeros((HEADS,), jnp.float32),
            jnp.zeros((HEADS, HDIM, HDIM), jnp.bfloat16),
        )

    shaped_q, inside, growth, fade, update = lax.cond(is_self, local_blocks, skip_blocks, 0)

    gains = jnp.concatenate([query_gain, out_gain, jnp.zeros((6, HD), jnp.float32)], axis=0)
    meta = jnp.zeros((8, 128), jnp.int32)
    meta = meta.at[0, :64].set(cache_pos).at[0, 64].set(span_start[0])
    fade_tile = jnp.zeros((8, 128), jnp.float32).at[0, :HEADS].set(fade)
    k, v, metas, q, at_x, at_gain, updates, fades = exchange(
        inputs, gains, cache_kv, meta, update, fade_tile
    )
    metas = metas[:, 0, :]
    pos = metas[:, :64].reshape(1, KEYS)
    y_from = jnp.where(y < 2, 3 - y, y)
    begins = metas[:, 64].reshape(4, 4, 2)
    begins = lax.dynamic_index_in_dim(begins, y_from, 1, False)
    begins = lax.dynamic_index_in_dim(begins, core, 1, False)
    starts = jnp.stack([begins[0], begins[2], jnp.where(y < 2, 1, 0).astype(jnp.int32)])

    o, lse = attend(starts, pos, q, k, v)

    kept = lax.dynamic_slice_in_dim(state_in[0], seq_at * 16, 16, 1)

    def scan(unused):
        entering = []
        now = kept
        for at in range(8):
            entering.append(now.astype(jnp.bfloat16))
            now = fades[at, 0, :HEADS][:, None, None] * now + updates[at].astype(jnp.float32)
        return jnp.stack(entering), now

    def no_scan(unused):
        return jnp.zeros((8, HEADS, 16, HDIM), jnp.bfloat16), kept

    entering, state_local = lax.cond(is_self, scan, no_scan, 0)

    o_parts, lses, entered = returning(o, lse, entering)

    lses = jnp.transpose(lses[..., :5], (0, 2, 1, 3)).reshape(4, HALF, HEADS)
    factor = jnp.exp(lses - jnp.max(lses, axis=0))
    factor = factor / jnp.sum(factor, axis=0)
    shaped = o_parts.reshape(4, HALF, HEADS, HDIM).astype(jnp.float32)
    attended = jnp.sum(shaped * factor[..., None], axis=0).reshape(HALF, HD)
    att = (at_x.astype(jnp.float32) + attended * at_gain[1]).astype(jnp.bfloat16)

    def self_mix(unused):
        carried_in = jnp.einsum(
            "thd,hde->the", shaped_q, entered, preferred_element_type=jnp.float32
        )
        mixed = rms_rows(inside + carried_in * growth[:, :, None]).reshape(128, HD)
        return (inputs.astype(jnp.float32) + mixed * out_gain[0]).astype(jnp.bfloat16)

    def no_mix(unused):
        return jnp.zeros((128, HD), jnp.bfloat16)

    mix = lax.cond(is_self, self_mix, no_mix, 0)
    section_output, fresh = onward(att, mix)
    rows = lax.dynamic_slice_in_dim(fresh, (section_at % 2) * 8, 8, 0)
    nfresh = rms_rows(rows.astype(jnp.float32))
    global_new = jnp.concatenate(
        [nfresh * global_gain[0], nfresh * global_gain[1]], axis=1
    ).astype(jnp.bfloat16)
    return (section_output[None], state_local[None], global_new[None, None])


def solution(mesh):
    return jax.shard_map(
        local,
        mesh=mesh,
        in_specs=(
            P("section", "seq", None),
            P("section", None, None, None),
            P(),
            P("section", None),
            P("section", "seq", None),
            P("section", None),
            P("section", None),
            P("section", None),
            P(),
            P(("section", "seq"), None),
            P(("section", "seq")),
            P("section"),
        ),
        out_specs=(
            P("section", "seq", None),
            P("section", None, "seq", None),
            P("seq", "section", None, None),
        ),
        check_vma=False,
    )
```

time: 801 us -> 225 us (0.28)
  the two profiles are of different devices: /device:TPU:17 before, /device:TPU:11 now
where the time goes in v1:
time: 225 us; the launch traced here: 224 us
  Pallas kernels  152 us (68%)
  local copies, waits for them, and re-layouts  34.6 us (15%)
  other arithmetic  27.5 us (12%)
  matrix products  8.03 us (4%)
    pallas_call x1, Pallas kernels, exchange(): pl.pallas_call(exchange_kernel, out_shape=(jax.ShapeDtypeStruct((KEYS, GR...  66.6 us
    pallas_call x1, Pallas kernels, returning(): pl.pallas_call(returning_kernel, out_shape=(jax.ShapeDtypeStruct((4, HALF...  32.9 us
    pallas_call x1, Pallas kernels, attend(): pl.pallas_call(attend_kernel, out_shape=(jax.ShapeDtypeStruct((1024, GROU...  28.5 us
    pallas_call x1, Pallas kernels, onward(): pl.pallas_call(onward_kernel, out_shape=(jax.ShapeDtypeStruct((128, HD),...  24.5 us
    unnamed x37, local copies, waits for them, and re-layouts  12.8 us
    another operation x7, local copies, waits for them, and re-layouts  8.09 us
    cond x7, other arithmetic  6.56 us
    mul x2, local copies, waits for them, and re-layouts, local(): attended = jnp.sum(shaped * factor[..., None], axis=0).reshape(HALF, HD)  6.42 us

profile of v1, /device:TPU:11, one launch (start us, length us, event | category | flops | bytes accessed | tf_op | source)
XLA Modules:
  0.0 224.3 jit_solution(7621731838590751096)
XLA Ops:
  0.8 14.0 %conditional.3 = (bf16[128,20,128]{0,2,1:T(8,128)(2,1)}, f32[128,20,128]{2,0,1:T(8,128)}, f32[128,20]{1,0:T(8,128)S(1)}, bf16[20,128,128]{2,1,0:T(8,128)(2,1)}, f32[8,128]{1,0:T(8,128)S(1)}) conditional(s32[]{:T(128)} %convert_element_type.125, () %tuple.44, (bf16[128,2560]{1,0:T(8,128)(2,1)}, f32[1,2560]{1,0:T(1,128)}, f32[1,2560]{1,0:T(1,128)}, ...), branch_computations={%region_1.2_spmd, %region_2.6_spmd} | conditional | flops 257904176 | bytes 18729880 | solution.py:547
  0.8 1.6 copy.74
  2.4 0.8 copy-done.12
  3.2 0.4 fusion.18
  3.7 3.2 %fusion.17 = (bf16[128,2560]{0,1:T(8,128)(2,1)}, bf16[128,2560]{0,1:T(8,128)(2,1)}) fusion(bf16[128,2560]{0,1:T(8,128)(2,1)} %copy-done.12, f32[2560]{0:T(1024)S(1)} %reduce.15, f32[128]{0:T(128)S(1)} %add_rsqrt_fusion, f32[2560]{0:T(1024)S(1)} %reduce.14), kind=kLoop, calls=%fused_computation.42 | loop fusion | flops 1966080 | bytes 1987072 | tf_op jit(solution)/shard_map/cond/branch_1_fun/convert_element_type | solution.py:530
  6.9 0.1 copy.75
  7.1 0.2 reduce_window_sum.10
  7.4 1.1 copy.76
  8.5 3.6 %convolution_bitcast_fusion = f32[128,20,128]{2,0,1:T(8,128)} fusion(bf16[128,20,128]{0,2,1:T(8,128)(2,1)} %bitcast.145, bf16[128,20,128]{0,2,1:T(8,128)(2,1)} %bitcast, bf16[128,20,128]{0,2,1:T(8,128)(2,1)} %bitcast.143, f32[20,128]{1,0:T(8,128)S(1)} %copy.69, pred[128,128]{1,0:T(8,128)(4,1)S(1)} %iota_compare_fusion), kind=kOutput, calls=%fused_computation.36 | convolution fusion | flops 169410560 | bytes 3303424 | tf_op jit(solution)/shard_map/cond/branch_1_fun/hts,shd->thd/dot_general | solution.py:486
  12.2 2.5 %convolution_convert_fusion = bf16[20,128,128]{2,1,0:T(8,128)(2,1)} fusion(bf16[128,20,128]{0,2,1:T(8,128)(2,1)} %bitcast.146, bf16[128,20,128]{0,2,1:T(8,128)(2,1)S(1)} %bitcast.144, f32[128,20]{0,1:T(8,128)S(1)} %copy.72), kind=kOutput, calls=%fused_computation.40 | convolution fusion | flops 85196800 | bytes 1976320 | tf_op jit(solution)/shard_map/cond/branch_1_fun/thd,the->hde/dot_general | solution.py:488
  14.7 0.7 fusion.39
  16.1 0.6 and_reduce_fusion
  16.7 2.5 %fusion.40 = s32[1,1]{1,0:T(1,128)} fusion(pred[1,1]{1,0:T(4,128)(4,1)} %bitcast.36, s32[1,1]{1,0:T(1,128)} %bitcast.138, s32[]{:T(128)} %bitcast.38, s32[]{:T(128)} %bitcast.39, s32[1,64]{1,0:T(1,128)S(1)} %bitcast.151), kind=kLoop, calls=%fused_computation.98 | loop fusion | flops 1 | bytes 273 | tf_op jit(solution)/shard_map/select.4
  19.2 2.0 scatter.18.meta_ref
  21.3 0.8 maximum_maximum_fusion.gain_ref
  22.1 66.6 %exchange.1 = (bf16[2048,640]{1,0:T(8,128)(2,1)S(1)}, bf16[2048,640]{1,0:T(8,128)(2,1)S(1)}, s32[32,8,128]{2,1,0:T(8,128)S(1)}, bf16[1024,640]{1,0:T(8,128)(2,1)...) custom-call(bf16[128,2560]{1,0:T(8,128)(2,1)} %bitcast.140, ...), custom_call_target="tpu_custom_call" | custom-call | tf_op jit(solution)/shard_map/exchange/pallas_call | solution.py:221
  88.8 1.5 copy-done.4
  90.3 1.5 copy-done.6
  91.8 1.1 copy-done.8
  92.9 0.2 slice_reduce_fusion
  93.1 0.1 reshape_squeeze.6
  93.2 0.7 constant_dynamic-slice_fusion
  93.8 1.3 pad_add_fusion.starts
  95.3 1.7 copy-done.5
  97.0 1.7 copy-done.7
  98.7 1.3 copy-done.9
  100.1 28.5 %attend.1 = (bf16[1024,640]{1,0:T(8,128)(2,1)S(1)}, f32[1024,128]{1,0:T(8,128)S(1)}) custom-call(s32[3]{0:T(128)S(1)} %pad_add_fusion.starts, s32[1,2048]{1,0:T(1,128)S(1)} %reshape.260.pos_ref, bf16[1024,640]{1,0:T(8,128)(2,1)S(1)} %copy-done.9, bf16[2048,640]{1,0:T(8,128)(2,1)S(1)} %copy-done.5, bf16[2048,640]{1,0:T(8,128)(2,1)S(1)} %copy-done.7), custom_call_target="tpu_custom_call" | custom-call | flops 5368709120 | bytes 10000000 | tf_op jit(solution)/shard_map/attend/pallas_call | solution.py:291
  128.6 1.1 copy-done.1
  129.6 0.8 copy-done.3
  130.4 0.7 dynamic-slice_bitcast_fusion
  131.1 9.1 %conditional.4 = (bf16[8,20,16,128]{3,2,1,0:T(8,128)(2,1)}, f32[20,16,128]{2,1,0:T(8,128)}) conditional(s32[]{:T(128)} %convert_element_type.125, f32[20,16,128]{2,1,0:T(8,128)} %dynamic-slice_bitcast_fusion, (f32[20,16,128]{2,1,0:T(8,128)}, f32[8,8,128]{2,1,0:T(8,128)S(1)}, bf16[8,20,16,128]{3,2,1,0:T(8,128)(2,1)S(1)}) %tuple.46), branch_computations={%region_6.7_spmd, %region_7.8_spmd} | conditional | flops 1802239 | bytes 4098256 | solution.py:579
  131.1 1.2 convert_add_fusion
  132.3 1.6 bitcast_dynamic-update-slice_fusion.3
  133.8 1.6 fusion.11
  135.5 0.6 bitcast_dynamic-update-slice_fusion.2
  136.1 0.7 fusion.9
  136.8 0.6 bitcast_dynamic-update-slice_fusion.1
  137.5 0.7 fusion.7
  138.2 0.6 bitcast_dynamic-update-slice_fusion
  138.8 0.7 fusion.5
  139.5 0.7 copy.116
  140.2 32.9 %returning.1 = (bf16[4,64,2560]{2,1,0:T(8,128)(2,1)}, f32[4,4,64,128]{3,2,1,0:T(8,128)}, bf16[20,128,128]{2,1,0:T(8,128)(2,1)S(1)}) custom-call(bf16[1024,640]{1,0:T(8,128)(2,1)} %copy-done.1, f32[1024,128]{1,0:T(8,128)} %copy-done.3, bf16[8,20,16,128]{3,2,1,0:T(8,128)(2,1)} %get-tuple-element.138.enter_ref), custom_call_target="tpu_custom_call" | custom-call | tf_op jit(solution)/shard_map/returning/pallas_call | solution.py:371
  173.1 12.0 %conditional.5 = (bf16[128,2560]{1,0:T(8,128)(2,1)}) conditional(s32[]{:T(128)} %convert_element_type.125, () %tuple.47, (bf16[128,2560]{1,0:T(8,128)(2,1)S(1)}, bf16[20,128,128]{2,1,0:T(8,128)(2,1)S(1)}, bf16[128,20,128]{0,2,1:T(8,128)(2,1)}, f32[128,20]{1,0:T(8,128)}, f32[128,20,128]{2,0,1:T(8,128)}, /*index=5*/f32[1,2560]{1,0:T(1,128)}) %tuple.88), branch_computations={%region_11.12_spmd, %region_12.14_spmd} | conditional | flops 86837760 | bytes 14520332 | solution.py:600
  173.1 2.8 %copy.85 = f32[128,20,128]{0,2,1:T(8,128)} copy(f32[128,20,128]{2,0,1:T(8,128)} %get-tuple-element.211) | data formatting | bytes 2621440 | tf_op jit(solution)/shard_map
  176.0 1.5 copy.84
  177.5 1.9 multiply_reduce_fusion
  179.4 1.2 broadcast_multiply_fusion
  180.6 0.3 copy.81
  180.9 1.3 reduce.16
  182.2 1.7 fusion.28
  184.0 1.1 copy.94
  185.3 0.1 copy.79
  185.4 0.2 copy.77
  185.6 0.1 copy.78
  185.8 0.1 copy.80
  185.9 2.2 mul.210
  188.1 4.3 %mul.211 = f32[4,64,2560]{2,1,0:T(8,128)} reshape(f32[4,64,20,128]{3,2,1,0:T(8,128)} %mul.210) | data formatting | bytes 5242880 | tf_op jit(solution)/shard_map/mul | solution.py:587
  192.3 2.2 multiply_reduce_fusion.1
  194.6 0.8 add_convert_fusion.att_ref
  195.4 24.5 %onward.1 = (bf16[128,2560]{1,0:T(8,128)(2,1)}, bf16[16,2560]{1,0:T(8,128)(2,1)}) custom-call(bf16[64,2560]{1,0:T(8,128)(2,1)} %add_convert_fusion.att_ref, bf16[128,2560]{1,0:T(8,128)(2,1)} %get-tuple-element.213.mix_ref), custom_call_target="tpu_custom_call" | custom-call | tf_op jit(solution)/shard_map/onward/pallas_call | solution.py:458
  219.9 0.9 fusion.33
  220.8 0.9 fusion.35
  221.7 0.6 pad_maximum_fusion
  222.4 2.0 copy.121
  (73 shorter events, 1.0 us)
Async XLA Ops:
  0.6 129.8 %copy-start = (f32[1,20,128,128]{3,2,1,0:T(8,128)S(1)}, f32[1,20,128,128]{3,2,1,0:T(8,128)}, u32[]{:S(2)}) copy-start(f32[1,20,128,128]{3,2,1,0:T(8,128)} %param.25) | copy-start | bytes 3932164
  0.7 15.4 %copy-start.25 = (s32[2]{0:T(128)S(1)}, s32[2]{0:T(128)}, u32[]{:S(2)}) copy-start(s32[2]{0:T(128)} %constant.166.clone.1) | copy-start | bytes 28
  0.7 16.0 %copy-start.22 = (s32[64]{0:T(128)S(1)}, s32[64]{0:T(128)}, u32[]{:S(2)}) copy-start(s32[64]{0:T(128)} %param.34) | copy-start | bytes 772
  0.7 20.6 %copy-start.18 = (f32[1,2560]{1,0:T(1,128)S(1)}, f32[1,2560]{1,0:T(1,128)}, u32[]{:S(2)}) copy-start(f32[1,2560]{1,0:T(1,128)} %param.31) | copy-start | bytes 30724
  0.7 21.4 %copy-start.2 = (bf16[64,5120]{1,0:T(8,128)(2,1)S(1)}, bf16[64,5120]{1,0:T(8,128)(2,1)}, u32[]{:S(2)}) copy-start(bf16[64,5120]{1,0:T(8,128)(2,1)} %kv_ref.1) | copy-start | bytes 1966084
  0.8 2.8 %copy-start.17 = (f32[1,2560]{1,0:T(1,128)S(1)}, f32[1,2560]{1,0:T(1,128)}, u32[]{:S(2)}) copy-start(f32[1,2560]{1,0:T(1,128)} %get-tuple-element.86) | copy-start | bytes 30724 | tf_op jit(solution)/shard_map/cond
  0.8 2.8 %copy-start.21 = (f32[1,2560]{1,0:T(1,128)S(1)}, f32[1,2560]{1,0:T(1,128)}, u32[]{:S(2)}) copy-start(f32[1,2560]{1,0:T(1,128)} %get-tuple-element.153) | copy-start | bytes 30724 | tf_op jit(solution)/shard_map/cond
  2.4 0.8 copy-start.12
  3.2 3.7 %copy-start.20 = (f32[1,128,20]{1,0,2:T(1,128)S(1)}, f32[1,128,20]{1,0,2:T(1,128)}, u32[]{:S(2)}) copy-start(f32[1,128,20]{1,0,2:T(1,128)} %get-tuple-element.205) | copy-start | bytes 30724 | tf_op jit(solution)/shard_map/cond
  3.2 3.8 %copy-start.24 = (f32[16]{0:T(128)S(1)}, f32[16]{0:T(128)}, u32[]{:S(2)}) copy-start(f32[16]{0:T(128)} %get-tuple-element.155) | copy-start | bytes 196 | tf_op jit(solution)/shard_map/cond
  3.2 3.8 %copy-start.23 = (s32[1,20]{1,0:T(1,128)S(1)}, s32[1,20]{1,0:T(1,128)}, u32[]{:S(2)}) copy-start(s32[1,20]{1,0:T(1,128)} %get-tuple-element.154) | copy-start | bytes 244 | tf_op jit(solution)/shard_map/cond
  3.6 3.8 %copy-start.11 = (bf16[1,128,2560]{2,1,0:T(8,128)(2,1)S(1)}, bf16[1,128,2560]{2,1,0:T(8,128)(2,1)}, u32[]{:S(2)}) copy-start(bf16[1,128,2560]{2,1,0:T(8,128)(2,1)} %get-tuple-element.206) | copy-start | bytes 1966084 | tf_op jit(solution)/shard_map/cond
  8.5 3.7 %copy-start.14 = (bf16[128,2560]{0,1:T(8,128)(2,1)S(1)}, bf16[128,2560]{0,1:T(8,128)(2,1)}, u32[]{:S(2)}) copy-start(bf16[128,2560]{0,1:T(8,128)(2,1)} %get-tuple-element.220) | copy-start | bytes 1966084 | tf_op jit(solution)/shard_map/cond
  14.7 6.6 %copy-start.16 = (f32[128,20]{1,0:T(8,128)}, f32[128,20]{1,0:T(8,128)S(1)}, u32[]{:S(2)}) copy-start(f32[128,20]{1,0:T(8,128)S(1)} %get-tuple-element.144) | copy-start | bytes 30724
  88.8 1.5 copy-start.4
  90.3 1.5 copy-start.6
  91.8 1.1 copy-start.8
  95.2 1.7 copy-start.5
  97.0 1.7 copy-start.7
  98.7 1.3 copy-start.9
  128.5 1.1 copy-start.1
  129.6 0.8 copy-start.3
  140.2 32.9 %copy-start.10 = (bf16[1,128,2560]{2,1,0:T(8,128)(2,1)S(1)}, bf16[1,128,2560]{2,1,0:T(8,128)(2,1)}, u32[]{:S(2)}) copy-start(bf16[1,128,2560]{2,1,0:T(8,128)(2,1)} %param.24) | copy-start | bytes 1966084
  173.1 12.0 %copy-start.13 = (f32[4,4,64,128]{3,2,1,0:T(8,128)S(1)}, f32[4,4,64,128]{3,2,1,0:T(8,128)}, u32[]{:S(2)}) copy-start(f32[4,4,64,128]{3,2,1,0:T(8,128)} %get-tuple-element.140) | copy-start | bytes 1572868
  188.1 4.3 %copy-start.15 = (bf16[4,64,2560]{2,1,0:T(8,128)(2,1)S(1)}, bf16[4,64,2560]{2,1,0:T(8,128)(2,1)}, u32[]{:S(2)}) copy-start(bf16[4,64,2560]{2,1,0:T(8,128)(2,1)} %get-tuple-element.139) | copy-start | bytes 3932164
  194.5 26.3 %copy-start.19 = (f32[2,2560]{1,0:T(2,128)S(1)}, f32[2,2560]{1,0:T(2,128)}, u32[]{:S(2)}) copy-start(f32[2,2560]{1,0:T(2,128)} %param.32) | copy-start | bytes 61444

commit v2 on v0

v2 whole, which is shorter than its diff:
```python
import jax
import jax.numpy as jnp
from jax import lax
from jax.experimental import pallas as pl
from jax.experimental.pallas import tpu as pltpu
from jax.sharding import PartitionSpec as P

MESH = pl.DeviceIdType.MESH
EPSILON = 1e-06
MASKED_SCORE = -1e30
LOG2E = 1.4426950408889634
HD = 2560
HEADS = 20
HDIM = 128
GROUP = 640
LOCAL_HEADS = 5
HALF = 64
KEYS = 2048
QBLOCK = 256
KCHUNK = 512
STEP = HDIM ** (-0.5) * LOG2E


def device_at(y, x, z, core):
    return (y * 4 + (x // 2) * 2 + core, z * 2 + x % 2)


def shifted(value, by):
    return lax.rem(value + by + 4, 4)


def remote(src, dst, send_sem, recv_sem, peer):
    return pltpu.make_async_remote_copy(
        src_ref=src,
        dst_ref=dst,
        send_sem=send_sem,
        recv_sem=recv_sem,
        device_id=peer,
        device_id_type=MESH,
    )


def span_kernel(
    x_ref,
    state_ref,
    table_ref,
    rate_ref,
    gates_ref,
    gain_ref,
    key_gain_ref,
    global_ref,
    kv_ref,
    meta_ref,
    out_ref,
    state_out,
    global_out,
    at_x,
    at_gain,
    queries,
    kvbuf,
    metabuf,
    qbuf,
    scores_ref,
    pos_ref,
    o_out,
    lse_out,
    o_in,
    lse_in,
    r_att,
    decays,
    decays_t,
    inside,
    self_q,
    kept,
    update_out,
    fade_out,
    update_in,
    fade_in,
    enter_out,
    enter_in,
    r_self,
    fresh,
    h_send,
    h_recv,
    a_send,
    a_recv,
    a_local,
    b_send,
    b_recv,
    c_send,
    c_recv,
    qa_send,
    qa_recv,
    qa_local,
    qb_send,
    qb_recv,
    o_send,
    o_recv,
    o_local,
    u_send,
    u_recv,
    e_send,
    e_recv,
    s_local,
    r_send,
    r_recv,
    w_send,
    w_recv,
    f_send,
    f_recv,
):
    section = lax.axis_index("section")
    seq = lax.axis_index("seq")
    y, core = section // 4, section % 2
    x, z = ((section // 2) % 2) * 2 + seq % 2, seq // 2
    is_self = section < 8
    is_cross = jnp.logical_not(is_self)
    sibling = device_at(y, x, z, 1 - core)
    partner = device_at(3 - y, x, z, core)

    peers = [(lax.rem(section + by, 16), seq) for by in range(1, 16)]
    for dz in range(4):
        for dx in range(4):
            if (dz, dx) not in ((0, 0), (0, 2)):
                peers.append(device_at(y, shifted(x, dx), shifted(z, dz), core))
    barrier = pltpu.get_barrier_semaphore()
    for peer in peers:
        pl.semaphore_signal(barrier, inc=1, device_id=peer, device_id_type=MESH)
    pl.semaphore_wait(barrier, len(peers))

    waits_at_end = []

    half_copy = remote(x_ref.at[pl.ds(HALF, HALF)], at_x, h_send.at[0], h_recv.at[0], partner)
    gain_copy = remote(gain_ref, at_gain, h_send.at[1], h_recv.at[1], partner)

    @pl.when(is_cross)
    def _():
        half_copy.start()
        gain_copy.start()

    META = LOCAL_HEADS

    def kv_source(item, kind, to_x):
        if item == META:
            return meta_ref
        column = to_x * GROUP + item * HDIM + kind * HD
        return kv_ref.at[:, pl.ds(pl.multiple_of(column, HDIM), HDIM)]

    def kv_landing(item, kind, from_x):
        if item == META:
            return metabuf.at[y * 8 + core * 4 + from_x]
        rows = pl.ds(pl.multiple_of(y * 512 + core * 256 + from_x * 64, 64), 64)
        return kvbuf.at[item, rows, pl.ds(kind * HDIM, HDIM)]

    def kinds(item):
        return (0,) if item == META else (0, 1)

    def kv_spread(item):
        for kind in kinds(item):
            pltpu.make_async_copy(
                kv_source(item, kind, x), kv_landing(item, kind, x), a_local.at[item, kind]
            ).start()
            for at, dx in enumerate((1, 3, 2)):
                to_x = shifted(x, dx)
                copy = remote(
                    kv_source(item, kind, to_x),
                    kv_landing(item, kind, x),
                    a_send.at[item, kind, at],
                    a_recv.at[item, kind, at],
                    device_at(y, to_x, z, core),
                )
                copy.start()
                waits_at_end.append(copy)

    def kv_block(item, from_y, from_core, part):
        start, count = ((0, 4), (0, 2), (2, 2))[part]
        if item == META:
            return metabuf.at[pl.ds(from_y * 8 + from_core * 4 + start, count)]
        rows = pl.ds(
            pl.multiple_of(from_y * 512 + from_core * 256 + start * 64, 64), count * 64
        )
        return kvbuf.at[item, rows]

    up, down = device_at(shifted(y, 1), x, z, core), device_at(shifted(y, 3), x, z, core)
    y_up, y_down, y_far = shifted(y, 1), shifted(y, 3), shifted(y, 2)

    def push(ref, sends, recvs, item, at, peer):
        copy = remote(ref, ref, sends.at[item, at], recvs.at[item, at], peer)
        copy.start()
        waits_at_end.append(copy)

    def arrived(ref, sends, recvs, item, at, peer):
        remote(ref, ref, sends.at[item, at], recvs.at[item, at], peer).wait_recv()

    def kv_own(item):
        for kind in kinds(item):
            pltpu.make_async_copy(
                kv_source(item, kind, x), kv_landing(item, kind, x), a_local.at[item, kind]
            ).wait()
            for at, dx in enumerate((1, 3, 2)):
                landed = kv_landing(item, kind, shifted(x, -dx))
                remote(
                    landed, landed, a_send.at[item, kind, at], a_recv.at[item, kind, at], sibling
                ).wait_recv()
        block = kv_block(item, y, core, 0)
        push(block, b_send, b_recv, item, 0, up)
        push(block, b_send, b_recv, item, 1, down)
        push(block, c_send, c_recv, item, 0, sibling)

    def kv_forward(item):
        block = kv_block(item, y_down, core, 0)
        arrived(block, b_send, b_recv, item, 0, up)
        push(kv_block(item, y_down, core, 1), b_send, b_recv, item, 2, up)
        push(block, c_send, c_recv, item, 1, sibling)
        block = kv_block(item, y_up, core, 0)
        arrived(block, b_send, b_recv, item, 1, down)
        push(kv_block(item, y_up, core, 2), b_send, b_recv, item, 3, down)
        push(block, c_send, c_recv, item, 2, sibling)

    def kv_far(item):
        for part in (1, 2):
            block = kv_block(item, y_far, core, part)
            arrived(block, b_send, b_recv, item, part + 1, up)
            push(block, c_send, c_recv, item, part + 2, sibling)

    def kv_ready(item):
        other = 1 - core
        for at, (from_y, part) in enumerate(
            ((y, 0), (y_down, 0), (y_up, 0), (y_far, 1), (y_far, 2))
        ):
            arrived(kv_block(item, from_y, other, part), c_send, c_recv, item, at, sibling)

    def q_source(item, to_x):
        return queries.at[:, pl.ds(pl.multiple_of(to_x * GROUP + item * HDIM, HDIM), HDIM)]

    def q_landing(item, from_x):
        return qbuf.at[item, pl.ds(pl.multiple_of(z * 256 + from_x * HALF, HALF), HALF)]

    def q_spread(item):
        pltpu.make_async_copy(q_source(item, x), q_landing(item, x), qa_local.at[item]).start()
        for at, dx in enumerate((1, 3, 2)):
            to_x = shifted(x, dx)
            copy = remote(
                q_source(item, to_x),
                q_landing(item, x),
                qa_send.at[item, at],
                qa_recv.at[item, at],
                device_at(y, to_x, z, core),
            )
            copy.start()
            waits_at_end.append(copy)

    z_up, z_down, z_far = shifted(z, 1), shifted(z, 3), shifted(z, 2)
    right, left = device_at(y, x, z_up, core), device_at(y, x, z_down, core)

    def q_block(item, from_z, part):
        start, count = ((0, 256), (0, 128), (128, 128))[part]
        return qbuf.at[item, pl.ds(pl.multiple_of(from_z * 256 + start, 128), count)]

    def q_own(item):
        pltpu.make_async_copy(q_source(item, x), q_landing(item, x), qa_local.at[item]).wait()
        for at, dx in enumerate((1, 3, 2)):
            landed = q_landing(item, shifted(x, -dx))
            arrived(landed, qa_send, qa_recv, item, at, right)
        push(q_block(item, z, 0), qb_send, qb_recv, item, 0, right)
        push(q_block(item, z, 0), qb_send, qb_recv, item, 1, left)

    def q_forward(item):
        arrived(q_block(item, z_down, 0), qb_send, qb_recv, item, 0, right)
        push(q_block(item, z_down, 1), qb_send, qb_recv, item, 2, right)
        arrived(q_block(item, z_up, 0), qb_send, qb_recv, item, 1, left)
        push(q_block(item, z_up, 2), qb_send, qb_recv, item, 3, left)

    def q_ready(item):
        arrived(q_block(item, z_far, 1), qb_send, qb_recv, item, 2, right)
        arrived(q_block(item, z_far, 2), qb_send, qb_recv, item, 3, left)

    state_rows = pltpu.make_async_copy(
        state_ref.at[:, pl.ds(pl.multiple_of(seq * 16, 16), 16), :], kept, s_local.at[0]
    )
    state_rows.start()
    lanes = lax.broadcasted_iota(jnp.int32, (128, 128), 1)
    sublanes = lax.broadcasted_iota(jnp.int32, (128, 128), 0)
    causal = sublanes >= lanes

    def inverse_rms(values):
        return lax.rsqrt(jnp.mean(values * values, axis=1, keepdims=True) + EPSILON)

    def decay_column(head):
        return jnp.sum(jnp.where(lanes == head, decays[...], 0.0), axis=1, keepdims=True)

    def decay_setup():
        picked = jnp.zeros((1, HEADS), jnp.float32)
        for entry in range(16):
            picked = jnp.where(rate_ref[...] == entry, table_ref[entry], picked)
        decays[...] = jnp.zeros((128, 128), jnp.float32)
        decays[:, 0:HEADS] = jnp.log(picked) + jnp.log(gates_ref[...])
        summed = jnp.dot(
            jnp.where(causal, 1.0, 0.0),
            decays[...],
            precision=lax.Precision.HIGHEST,
            preferred_element_type=jnp.float32,
        )
        decays[...] = summed
        turned = jnp.transpose(summed)
        decays_t[...] = turned
        fade_out[...] = jnp.broadcast_to(jnp.exp(turned[:, 127:128])[0:24], (24, 128))

    def retain(first, last):
        scale = inverse_rms(x_ref[...].astype(jnp.float32))

        def one(head, carry):
            columns = pl.ds(pl.multiple_of(head * HDIM, HDIM), HDIM)
            values = x_ref[:, columns]
            normed = values.astype(jnp.float32) * scale
            query = (normed * gain_ref[0:1, columns]).astype(jnp.bfloat16)
            key_rows = (normed * key_gain_ref[:, columns]).astype(jnp.bfloat16)
            self_q[:, columns] = query
            products = lax.dot_general(
                query, key_rows, (((1,), (1,)), ((), ())), preferred_element_type=jnp.float32
            )
            column = decay_column(head)
            row = decays_t[pl.ds(head, 1), :]
            weights = jnp.where(
                causal, products * jnp.exp(jnp.where(causal, column - row, 0.0)), 0.0
            ).astype(jnp.bfloat16)
            inside[:, columns] = jnp.dot(weights, values, preferred_element_type=jnp.float32)
            fading = jnp.exp(row[:, 127:128] - column)
            faded = (key_rows.astype(jnp.float32) * fading).astype(jnp.bfloat16)
            update_out[pl.ds(head, 1)] = lax.dot_general(
                faded, values, (((0,), (0,)), ((), ())), preferred_element_type=jnp.float32
            ).astype(jnp.bfloat16)[None]
            return carry

        lax.fori_loop(first, last, one, 0)

    def seq_peer(at):
        to_z, to_x = shifted(z, at // 2), (x // 2) * 2 + lax.rem(x + at % 2, 2)
        return to_z * 2 + to_x % 2, device_at(y, to_x, to_z, core)

    def update_copies():
        copies = []
        for at in range(8):
            to_seq, peer = seq_peer(at)
            rows = pl.ds(pl.multiple_of(to_seq * 16, 16), 16)
            pairs = (
                (update_out.at[:, rows, :], update_in.at[seq]),
                (fade_out, fade_in.at[seq]),
            )
            for kind, (src, dst) in enumerate(pairs):
                if at == 0:
                    copies.append(pltpu.make_async_copy(src, dst, s_local.at[1 + kind]))
                else:
                    copies.append(
                        remote(src, dst, u_send.at[at, kind], u_recv.at[at, kind], peer)
                    )
        return copies

    def enter_copies():
        copies = []
        for at in range(8):
            to_seq, peer = seq_peer(at)
            dst = enter_in.at[:, pl.ds(pl.multiple_of(seq * 16, 16), 16), :]
            if at == 0:
                copies.append(pltpu.make_async_copy(enter_out.at[to_seq], dst, s_local.at[3]))
            else:
                copies.append(
                    remote(enter_out.at[to_seq], dst, e_send.at[at], e_recv.at[at], peer)
                )
        return copies

    def scan():
        def one(head, carry):
            now = kept[pl.ds(head, 1)][0]
            for at in range(8):
                enter_out[at, pl.ds(head, 1)] = now.astype(jnp.bfloat16)[None]
                fade = fade_in[at, pl.ds(head, 1), :]
                now = fade * now + update_in[at, pl.ds(head, 1)][0].astype(jnp.float32)
            state_out[pl.ds(head, 1)] = now[None]
            return carry

        lax.fori_loop(0, HEADS, one, 0)

    def mix(first, last):
        def one(head, carry):
            columns = pl.ds(pl.multiple_of(head * HDIM, HDIM), HDIM)
            carried = jnp.dot(
                self_q[:, columns], enter_in[pl.ds(head, 1)][0], preferred_element_type=jnp.float32
            )
            retained = inside[:, columns] + jnp.exp(decay_column(head)) * carried
            mixed = retained * inverse_rms(retained)
            r_self[:, columns] = (
                x_ref[:, columns].astype(jnp.float32) + mixed * gain_ref[1:2, columns]
            ).astype(jnp.bfloat16)
            return carry

        lax.fori_loop(first, last, one, 0)

    after = (lax.rem(section + 1, 16), seq)

    def self_result(group):
        columns = pl.ds(group * GROUP, GROUP)
        return remote(
            r_self.at[:, columns], out_ref.at[:, columns], w_send.at[group], w_recv.at[group], after
        )

    def fresh_rows(to):
        return r_self.at[pl.ds(pl.multiple_of((to // 2) * 16, 16), 16)]

    own_fresh = pltpu.make_async_copy(fresh_rows(section), fresh, s_local.at[4])

    def fresh_copy(by):
        to = lax.rem(section + by, 16)
        return remote(fresh_rows(to), fresh, f_send.at[by], f_recv.at[0], (to, seq))

    is_root = section == 7

    half_at = jnp.where(is_self, 1, 0)
    y_from = jnp.where(is_self, 3 - y, y)

    def place_setup():
        lane = lax.broadcasted_iota(jnp.int32, (1, 128), 1)
        for pair in range(16):
            pos_ref[:, pair * 128 : (pair + 1) * 128] = jnp.where(
                lane < 64, metabuf[2 * pair, 0:1, :], metabuf[2 * pair + 1, 0:1, :]
            )

    def attend(item):
        index = lax.broadcasted_iota(jnp.int32, (QBLOCK, 128), 0)
        offset = ((index // 64) % 2) * 128 + half_at * HALF + index % 64
        first_tile = y_from * 8 + core * 4
        begin = jnp.where(
            index < 128, metabuf[first_tile][1:2, :], metabuf[first_tile + 2][1:2, :]
        )
        diagonal = lax.broadcasted_iota(jnp.int32, (QBLOCK, QBLOCK), 0) == (
            lax.broadcasted_iota(jnp.int32, (QBLOCK, QBLOCK), 1)
        )

        def block(at, carry):
            rows = pl.ds(pl.multiple_of(at * QBLOCK, QBLOCK), QBLOCK)
            query = qbuf[item, rows, :]
            places = begin + offset + at * 256
            highest = jnp.full((QBLOCK, 128), MASKED_SCORE, jnp.float32)
            for chunk in range(KEYS // KCHUNK):
                keys = kvbuf[item, chunk * KCHUNK : (chunk + 1) * KCHUNK, 0:HDIM]
                scores = lax.dot_general(
                    query, keys, (((1,), (1,)), ((), ())), preferred_element_type=jnp.float32
                )
                for part in range(KCHUNK // 128):
                    here = slice(chunk * KCHUNK + part * 128, chunk * KCHUNK + (part + 1) * 128)
                    piece = jnp.where(
                        pos_ref[:, here] <= places,
                        scores[:, part * 128 : (part + 1) * 128],
                        MASKED_SCORE,
                    )
                    scores_ref[:, here] = piece
                    highest = jnp.maximum(highest, piece)
            top = jnp.max(highest, axis=1, keepdims=True)
            totals = jnp.zeros((QBLOCK, 128), jnp.float32)
            pieces = jnp.zeros((QBLOCK, HDIM), jnp.float32)
            for chunk in range(KEYS // KCHUNK):
                here = slice(chunk * KCHUNK, (chunk + 1) * KCHUNK)
                likely = jnp.exp2((scores_ref[:, here] - top) * STEP)
                for part in range(KCHUNK // 128):
                    totals += likely[:, part * 128 : (part + 1) * 128]
                pieces += jnp.dot(
                    likely.astype(jnp.bfloat16),
                    kvbuf[item, here, HDIM : 2 * HDIM],
                    preferred_element_type=jnp.float32,
                )
            total = jnp.sum(totals, axis=1, keepdims=True)
            o_out[item, rows, :] = (pieces / total).astype(jnp.bfloat16)
            lse = top * HDIM ** (-0.5) + jnp.log(total)
            flat = jnp.sum(jnp.where(diagonal, lse, 0.0), axis=0, keepdims=True)
            for pair in range(2):
                lse_out[item, at, pair] = jnp.broadcast_to(
                    flat[:, pair * 128 : (pair + 1) * 128], (8, 128)
                )
            return carry

        lax.fori_loop(0, 4, block, 0)

    ORDER = [(dz, dx) for dz in (2, 1, 3, 0) for dx in (2, 1, 3, 0)]

    def piece_copies(item):
        copies = []
        for at, (dz, dx) in enumerate(ORDER):
            to_x, to_z = shifted(x, dx), shifted(z, dz)
            rows = pl.ds(pl.multiple_of(to_z * 256 + to_x * HALF, HALF), HALF)
            pairs = (
                (lse_out.at[item, to_z, to_x // 2], lse_in.at[item, z, x]),
                (o_out.at[item, rows], o_in.at[item, z, x]),
            )
            for kind, (src, dst) in enumerate(pairs):
                if (dz, dx) == (0, 0):
                    copies.append(pltpu.make_async_copy(src, dst, o_local.at[item, kind]))
                else:
                    copies.append(
                        remote(
                            src,
                            dst,
                            o_send.at[item, at, kind],
                            o_recv.at[item, at, kind],
                            device_at(y, to_x, to_z, core),
                        )
                    )
        return copies

    def pieces_back(item):
        for copy in piece_copies(item):
            copy.start()

    helped = jnp.where(section < 4, section + 12, section + 4)
    att_target = (jnp.where(is_self, lax.rem(helped + 1, 16), lax.rem(section + 1, 16)), seq)
    att_rows = pl.ds(pl.multiple_of(half_at * HALF, HALF), HALF)

    def att_result(item, group):
        columns = pl.ds(group * GROUP + item * HDIM, HDIM)
        return remote(
            r_att.at[:, columns],
            out_ref.at[att_rows, columns],
            r_send.at[item, group],
            r_recv.at[half_at, item, group],
            att_target,
        )

    def merge(item):
        for copy in piece_copies(item):
            copy.wait()
        row = lax.broadcasted_iota(jnp.int32, (HALF, 128), 0)
        lane = lax.broadcasted_iota(jnp.int32, (HALF, 128), 1)
        mine = lane == row + (x % 2) * HALF
        for group in range(4):
            sums = [
                jnp.sum(
                    jnp.where(mine, lse_in[item, from_z, group, 0:1, :], 0.0), axis=1, keepdims=True
                )
                for from_z in range(4)
            ]
            overall = jnp.maximum(jnp.maximum(sums[0], sums[1]), jnp.maximum(sums[2], sums[3]))
            shares = [jnp.exp(value - overall) for value in sums]
            whole = shares[0] + shares[1] + shares[2] + shares[3]
            attended = jnp.zeros((HALF, HDIM), jnp.float32)
            for from_z in range(4):
                attended += shares[from_z] * o_in[item, from_z, group].astype(jnp.float32)
            attended = attended / whole
            here = slice(group * GROUP + item * HDIM, group * GROUP + (item + 1) * HDIM)
            r_att[:, here] = (
                at_x[:, here].astype(jnp.float32) + attended * at_gain[1:2, here]
            ).astype(jnp.bfloat16)
            att_result(item, group).start()

    kv_spread(META)
    for item in range(LOCAL_HEADS):
        kv_spread(item)

    @pl.when(is_cross)
    def _():
        at_x[...] = x_ref[0:HALF, :]
        at_gain[...] = gain_ref[...]

    @pl.when(is_self)
    def _():
        decay_setup()
        half_copy.wait_recv()
        gain_copy.wait_recv()

    rows = at_x[...].astype(jnp.float32)
    queries[...] = (rows * inverse_rms(rows) * at_gain[0:1, :]).astype(jnp.bfloat16)
    for item in range(LOCAL_HEADS):
        q_spread(item)
    kv_own(META)
    kv_own(0)
    kv_own(1)

    @pl.when(is_self)
    def _():
        retain(0, 7)

    for item in range(LOCAL_HEADS):
        q_own(item)
    kv_forward(META)
    kv_forward(0)
    kv_own(2)

    @pl.when(is_self)
    def _():
        retain(7, 14)

    for item in range(LOCAL_HEADS):
        q_forward(item)
    kv_far(META)
    kv_far(0)
    kv_forward(1)
    kv_own(3)

    @pl.when(is_self)
    def _():
        retain(14, HEADS)
        for copy in update_copies():
            copy.start()

    kv_ready(META)
    place_setup()
    for item in range(LOCAL_HEADS):
        q_ready(item)
    kv_far(1)
    kv_forward(2)
    kv_own(4)
    kv_ready(0)
    attend(0)
    pieces_back(0)

    kv_far(2)
    kv_forward(3)
    kv_ready(1)
    attend(1)
    pieces_back(1)

    state_rows.wait()

    @pl.when(is_self)
    def _():
        for copy in update_copies():
            copy.wait()
        scan()
        for copy in enter_copies():
            copy.start()

    @pl.when(is_cross)
    def _():
        state_out[...] = kept[...]

    kv_far(3)
    kv_forward(4)
    kv_ready(2)
    merge(0)
    attend(2)
    pieces_back(2)

    kv_far(4)
    kv_ready(3)
    merge(1)
    attend(3)
    pieces_back(3)

    @pl.when(is_self)
    def _():
        for copy in enter_copies():
            copy.wait()
        mix(0, HEADS)
        for group in range(4):
            self_result(group).start()

    @pl.when(is_root)
    def _():
        own_fresh.start()
        for by in range(1, 16):
            fresh_copy(by).start()

    kv_ready(4)
    merge(2)
    attend(4)
    pieces_back(4)
    merge(3)

    @pl.when(is_root)
    def _():
        own_fresh.wait()

    @pl.when(jnp.logical_not(is_root))
    def _():
        fresh_copy(1).wait_recv()

    both = fresh[...].astype(jnp.float32)
    new_rows = jnp.where(core == 0, both[0:8], both[8:16])
    new_rows = new_rows * inverse_rms(new_rows)
    global_out[:, 0:HD] = (new_rows * global_ref[0:1, :]).astype(jnp.bfloat16)
    global_out[:, HD : 2 * HD] = (new_rows * global_ref[1:2, :]).astype(jnp.bfloat16)
    merge(4)

    from_self = jnp.logical_and(section >= 1, section <= 8)

    @pl.when(from_self)
    def _():
        for group in range(4):
            self_result(group).wait_recv()

    @pl.when(jnp.logical_not(from_self))
    def _():
        for half in range(2):
            for item in range(LOCAL_HEADS):
                for group in range(4):
                    columns = pl.ds(group * GROUP + item * HDIM, HDIM)
                    landed = out_ref.at[pl.ds(half * HALF, HALF), columns]
                    remote(
                        landed,
                        landed,
                        r_send.at[item, group],
                        r_recv.at[half, item, group],
                        att_target,
                    ).wait_recv()

    for item in range(LOCAL_HEADS):
        for group in range(4):
            att_result(item, group).wait_send()
    for copy in waits_at_end:
        copy.wait_send()

    @pl.when(is_cross)
    def _():
        half_copy.wait_send()
        gain_copy.wait_send()

    @pl.when(is_self)
    def _():
        for group in range(4):
            self_result(group).wait_send()

    @pl.when(is_root)
    def _():
        for by in range(1, 16):
            fresh_copy(by).wait_send()


def span(*arguments):
    vmem = pl.BlockSpec(memory_space=pltpu.VMEM)
    smem = pl.BlockSpec(memory_space=pltpu.SMEM)
    hbm = pl.BlockSpec(memory_space=pl.ANY)
    dma = pltpu.SemaphoreType.DMA
    items = LOCAL_HEADS + 1

    def bf16(*shape):
        return pltpu.VMEM(shape, jnp.bfloat16)

    def f32(*shape):
        return pltpu.VMEM(shape, jnp.float32)

    return pl.pallas_call(
        span_kernel,
        out_shape=(
            jax.ShapeDtypeStruct((128, HD), jnp.bfloat16),
            jax.ShapeDtypeStruct((HEADS, 16, HDIM), jnp.float32),
            jax.ShapeDtypeStruct((8, 2 * HD), jnp.bfloat16),
        ),
        in_specs=[vmem, hbm, smem, vmem, vmem, vmem, vmem, vmem, hbm, hbm],
        out_specs=(vmem, vmem, vmem),
        scratch_shapes=[
            bf16(HALF, HD),
            f32(8, HD),
            bf16(HALF, HD),
            bf16(LOCAL_HEADS, KEYS, 2 * HDIM),
            pltpu.VMEM((32, 8, 128), jnp.int32),
            bf16(LOCAL_HEADS, 1024, HDIM),
            f32(QBLOCK, KEYS),
            pltpu.VMEM((1, KEYS), jnp.int32),
            bf16(LOCAL_HEADS, 1024, HDIM),
            f32(LOCAL_HEADS, 4, 2, 8, 128),
            bf16(LOCAL_HEADS, 4, 4, HALF, HDIM),
            f32(LOCAL_HEADS, 4, 4, 8, 128),
            bf16(HALF, HD),
            f32(128, 128),
            f32(128, 128),
            f32(128, HD),
            bf16(128, HD),
            f32(HEADS, 16, HDIM),
            bf16(HEADS, HDIM, HDIM),
            f32(24, 128),
            bf16(8, HEADS, 16, HDIM),
            f32(8, 24, 128),
            bf16(8, HEADS, 16, HDIM),
            bf16(HEADS, HDIM, HDIM),
            bf16(128, HD),
            bf16(16, HD),
            dma((2,)),
            dma((2,)),
            dma((items, 2, 3)),
            dma((items, 2, 3)),
            dma((items, 2)),
            dma((items, 4)),
            dma((items, 4)),
            dma((items, 5)),
            dma((items, 5)),
            dma((LOCAL_HEADS, 3)),
            dma((LOCAL_HEADS, 3)),
            dma((LOCAL_HEADS,)),
            dma((LOCAL_HEADS, 4)),
            dma((LOCAL_HEADS, 4)),
            dma((LOCAL_HEADS, 16, 2)),
            dma((LOCAL_HEADS, 16, 2)),
            dma((LOCAL_HEADS, 2)),
            dma((8, 2)),
            dma((8, 2)),
            dma((8,)),
            dma((8,)),
            dma((5,)),
            dma((LOCAL_HEADS, 4)),
            dma((2, LOCAL_HEADS, 4)),
            dma((4,)),
            dma((4,)),
            dma((16,)),
            dma((1,)),
        ],
        compiler_params=pltpu.CompilerParams(
            collective_id=0, has_side_effects=True, vmem_limit_bytes=48 * 1024 * 1024
        ),
        name="span",
    )(*arguments)


def local(
    section_input,
    state_in,
    decay_table,
    head_rate,
    gates,
    query_gain,
    key_gain,
    out_gain,
    global_gain,
    cache_kv,
    cache_pos,
    span_start,
):
    gains = jnp.concatenate([query_gain, out_gain, jnp.zeros((6, HD), jnp.float32)], axis=0)
    rows = jnp.concatenate([cache_pos, cache_pos])[None]
    begin = jnp.broadcast_to(span_start[:, None], (7, 128))
    meta = jnp.concatenate([rows, begin], axis=0)
    section_output, state_out, global_new = span(
        section_input[0],
        state_in[0],
        decay_table,
        head_rate,
        gates[0],
        gains,
        key_gain,
        global_gain,
        cache_kv,
        meta,
    )
    return (section_output[None], state_out[None], global_new[None, None])


def solution(mesh):
    return jax.shard_map(
        local,
        mesh=mesh,
        in_specs=(
            P("section", "seq", None),
            P("section", None, None, None),
            P(),
            P("section", None),
            P("section", "seq", None),
            P("section", None),
            P("section", None),
            P("section", None),
            P(),
            P(("section", "seq"), None),
            P(("section", "seq")),
            P("section"),
        ),
        out_specs=(
            P("section", "seq", None),
            P("section", None, "seq", None),
            P("seq", "section", None, None),
        ),
        check_vma=False,
    )
```

time: 801 us -> 108 us (0.13); the launches traced: 790 us -> 107 us
  waiting for transfers between devices: 320 us -> 0 us
  matrix products: 163 us -> 0 us
  blocking collectives: 139 us -> 0 us
  Pallas kernels: 0 us -> 94.7 us
  local copies, waits for them, and re-layouts: 78.7 us -> 9.25 us
  other arithmetic: 41.1 us -> 1.6 us
  starting transfers between devices: 19.5 us -> 0 us
  loops' own time: 14.3 us -> 0 us
  between operations: 14.9 us -> 1.3 us
    all_gather x3 -> x0, waiting for transfers between devices: 173 us -> none  [the longest x1 88.5 us: local(): gathered_q = lax.all_gather(queries, 'seq', axis=0, tiled=True)]
    dot_general x40 -> x0, matrix products: 163 us -> none  [the longest x20 87.8 us: one_head(): jnp.dot(likely.astype(jnp.bfloat16), value_head, preferred_element_type=j...]
    psum x1 -> x0, waiting for transfers between devices: 136 us -> none  [from_root(): return lax.psum(kept, axis)]
    all_gather x1 -> x0, blocking collectives: 122 us -> none  [prefix(): gathered = jax.tree.map(lambda a: lax.all_gather(a, axis), part)]
    pallas_call x0 -> x1, Pallas kernels: none -> 94.7 us  [span(): pl.pallas_call(span_kernel, out_shape=(jax.ShapeDtypeStruct((128, HD), jn...]
    dynamic_update_slice x40 -> x0, local copies, waits for them, and re-layouts: 29.3 us -> none  [attend_all(): return lax.map(one_head, jnp.arange(head_count, dtype=jnp.int32))]
    reduce_sum x24 -> x0, other arithmetic: 24.5 us -> none  [the longest x20 20.5 us: one_head(): totals = jnp.sum(likely, axis=1)]
    unnamed x1 -> x0, blocking collectives: 16.6 us -> none
  transfers between devices with their start and end apart: 9 -> 0, of which waited for: 6 -> 0; matrix products, arithmetic and copies ran while one was open for 35% -> 0% of each run, Pallas kernels for 0% -> 0%
where the time goes in v2:
time: 108 us; the launch traced here: 107 us
  Pallas kernels  94.7 us (88%)
  local copies, waits for them, and re-layouts  9.25 us (9%)
  other arithmetic  1.6 us (1%)
  between operations  1.3 us (1%)
    pallas_call x1, Pallas kernels, span(): pl.pallas_call(span_kernel, out_shape=(jax.ShapeDtypeStruct((128, HD), jn...  94.7 us
    unnamed x18, local copies, waits for them, and re-layouts  9.17 us

profile of v2, /device:TPU:17, one launch (start us, length us, event | category | flops | bytes accessed | tf_op | source)
XLA Modules:
  0.0 106.9 jit_solution(13512780352409442218)
XLA Ops:
  1.3 0.8 add_bitcast_fusion
  2.1 0.1 pad.5.clone
  2.2 0.8 copy.15
  3.0 0.8 maximum_maximum_fusion.gain_ref
  3.8 0.0 copy-start
  3.8 1.3 %copy-done = f32[1,20,128,128]{3,2,1,0:T(8,128)S(1)} copy-done((f32[1,20,128,128]{3,2,1,0:T(8,128)S(1)}, f32[1,20,128,128]{3,2,1,0:T(8,128)}, u32[]{:S(2)}) %copy-start) | copy-done | bytes 1310744
  5.1 0.0 copy-start.1
  5.1 1.1 %copy-done.1 = bf16[1,128,2560]{2,1,0:T(8,128)(2,1)S(1)} copy-done((bf16[1,128,2560]{2,1,0:T(8,128)(2,1)S(1)}, bf16[1,128,2560]{2,1,0:T(8,128)(2,1)}, u32[]{:S(2)}) %copy-start.1) | copy-done | bytes 655384
  6.2 0.0 copy-start.2
  6.2 1.1 %copy-done.2 = bf16[64,5120]{1,0:T(8,128)(2,1)S(1)} copy-done((bf16[64,5120]{1,0:T(8,128)(2,1)S(1)}, bf16[64,5120]{1,0:T(8,128)(2,1)}, u32[]{:S(2)}) %copy-start.2) | copy-done | bytes 655384
  7.3 0.0 copy-start.3
  7.3 0.7 copy-done.3
  8.0 0.0 copy-start.4
  8.0 0.7 copy-done.4
  8.7 0.0 copy-start.5
  8.7 0.7 copy-done.5
  9.3 0.0 copy-start.6
  9.3 0.7 copy-done.6
  10.0 94.7 %span.1 = (bf16[128,2560]{1,0:T(8,128)(2,1)S(1)}, f32[20,16,128]{2,1,0:T(8,128)S(1)}, bf16[8,5120]{1,0:T(8,128)(2,1)S(1)}) custom-call(bf16[128,2560]{1,0:T(8,128)(2,1)S(1)} %bitcast.12, f32[20,128,128]{2,1,0:T(8,128)S(1)} %bitcast.10, f32[16]{0:T(128)S(1)} %copy-done.5, s32[1,20]{1,0:T(1,128)S(1)} %copy-done.6, f32[128,20]{1,0:T(8,128)S(1)} %bitcast.13, ...), custom_call_target="tpu_custom_call" | custom-call | tf_op jit(solution)/shard_map/span/pallas_call | solution.py:739
  104.7 0.8 copy.20
  105.6 0.7 copy.21
  106.2 0.6 copy.22
  (2 shorter events, 0.0 us)
Async XLA Ops:
  3.8 1.3 %copy-start = (f32[1,20,128,128]{3,2,1,0:T(8,128)S(1)}, f32[1,20,128,128]{3,2,1,0:T(8,128)}, u32[]{:S(2)}) copy-start(f32[1,20,128,128]{3,2,1,0:T(8,128)} %param.13) | copy-start | bytes 3932164
  5.1 1.1 %copy-start.1 = (bf16[1,128,2560]{2,1,0:T(8,128)(2,1)S(1)}, bf16[1,128,2560]{2,1,0:T(8,128)(2,1)}, u32[]{:S(2)}) copy-start(bf16[1,128,2560]{2,1,0:T(8,128)(2,1)} %param.12) | copy-start | bytes 1966084
  6.2 1.1 %copy-start.2 = (bf16[64,5120]{1,0:T(8,128)(2,1)S(1)}, bf16[64,5120]{1,0:T(8,128)(2,1)}, u32[]{:S(2)}) copy-start(bf16[64,5120]{1,0:T(8,128)(2,1)} %kv_ref.1) | copy-start | bytes 1966084
  7.3 0.7 copy-start.3
  8.0 0.7 copy-start.4
  8.7 0.7 copy-start.5
  9.3 0.7 copy-start.6

commit v3 on v2

v3 whole, which is shorter than its diff:
```python
import jax
import jax.numpy as jnp
from jax import lax
from jax.experimental import pallas as pl
from jax.experimental.pallas import tpu as pltpu
from jax.sharding import PartitionSpec as P

MESH = pl.DeviceIdType.MESH
EPSILON = 1e-06
MASKED_SCORE = -1e30
LOG2E = 1.4426950408889634
HD = 2560
HEADS = 20
HDIM = 128
GROUP = 640
LOCAL_HEADS = 5
KEYS = 2048
TOKENS = 128
QBLOCK = 256
KCHUNK = 512
STEP = HDIM ** (-0.5) * LOG2E


def device_at(y, x, z, core):
    return (y * 4 + (x // 2) * 2 + core, z * 2 + x % 2)


def shifted(value, by):
    return lax.rem(value + by + 4, 4)


def remote(src, dst, send_sem, recv_sem, peer):
    return pltpu.make_async_remote_copy(
        src_ref=src,
        dst_ref=dst,
        send_sem=send_sem,
        recv_sem=recv_sem,
        device_id=peer,
        device_id_type=MESH,
    )


def span_kernel(
    x_hbm,
    state_ref,
    table_hbm,
    rate_hbm,
    gates_hbm,
    query_gain_hbm,
    key_gain_hbm,
    out_gain_hbm,
    global_hbm,
    kv_ref,
    positions_hbm,
    start_hbm,
    out_ref,
    state_out,
    global_out,
    x_ref,
    table_ref,
    start_ref,
    rate_ref,
    gates_ref,
    query_gain_ref,
    key_gain_ref,
    out_gain_ref,
    global_ref,
    positions_ref,
    i_local,
    queries,
    meta_ref,
    begin_ref,
    kvbuf,
    metabuf,
    beginbuf,
    qbuf,
    scores_ref,
    pos_ref,
    o_out,
    lse_out,
    o_in,
    lse_in,
    att_out,
    att_in,
    result,
    decays,
    decays_t,
    inside,
    kept,
    update_out,
    fade_out,
    update_in,
    fade_in,
    enter_out,
    enter_in,
    fresh,
    a_send,
    a_recv,
    a_local,
    b_send,
    b_recv,
    c_send,
    c_recv,
    qa_send,
    qa_recv,
    qa_local,
    qb_send,
    qb_recv,
    o_send,
    o_recv,
    t_send,
    t_recv,
    t_local,
    u_send,
    u_recv,
    e_send,
    e_recv,
    s_local,
    r_send,
    r_recv,
    w_send,
    w_recv,
    f_send,
    f_recv,
):
    section = lax.axis_index("section")
    seq = lax.axis_index("seq")
    y, core = section // 4, section % 2
    x, z = ((section // 2) % 2) * 2 + seq % 2, seq // 2
    is_self = section < 8
    is_cross = jnp.logical_not(is_self)
    is_root = section == 7
    sibling = device_at(y, x, z, 1 - core)
    other = device_at(y + 1 - 2 * (y % 2), x, z, core)
    partner = device_at(3 - y, x, z, core)
    after = (lax.rem(section + 1, 16), seq)
    before = (lax.rem(section + 15, 16), seq)

    fetches = [
        pltpu.make_async_copy(src, dst, i_local.at[at])
        for at, (src, dst) in enumerate(
            (
                (x_hbm, x_ref),
                (table_hbm, table_ref),
                (start_hbm, start_ref),
                (query_gain_hbm, query_gain_ref),
                (positions_hbm, positions_ref),
                (rate_hbm, rate_ref),
                (gates_hbm, gates_ref),
                (key_gain_hbm, key_gain_ref),
                (out_gain_hbm, out_gain_ref),
                (global_hbm, global_ref),
            )
        )
    ]
    for copy in fetches:
        copy.start()
    state_rows = pltpu.make_async_copy(
        state_ref.at[:, pl.ds(pl.multiple_of(seq * 16, 16), 16), :], kept, s_local.at[0]
    )
    state_rows.start()

    def seq_peer(at):
        to_z, to_x = shifted(z, at // 2), (x // 2) * 2 + lax.rem(x + at % 2, 2)
        return to_z * 2 + to_x % 2, device_at(y, to_x, to_z, core)

    peers = [sibling, other, partner]
    peers += [device_at(y, shifted(x, dx), z, core) for dx in (1, 2, 3)]
    peers += [seq_peer(at)[1] for at in range(2, 8)]
    barrier = pltpu.get_barrier_semaphore()
    for peer in peers + [before]:
        pl.semaphore_signal(barrier, inc=1, device_id=peer, device_id_type=MESH)

    @pl.when(jnp.logical_not(is_root))
    def _():
        pl.semaphore_signal(barrier, inc=1, device_id=(7, seq), device_id_type=MESH)

    waits_at_end = []

    META = LOCAL_HEADS

    def kinds(item):
        return (0,) if item == META else (0, 1)

    def kv_source(item, kind, to_x):
        if item == META:
            return meta_ref
        column = to_x * GROUP + item * HDIM + kind * HD
        return kv_ref.at[:, pl.ds(pl.multiple_of(column, HDIM), HDIM)]

    def kv_landing(item, kind, from_x):
        if item == META:
            return metabuf.at[z * 8 + core * 4 + from_x]
        rows = pl.ds(pl.multiple_of(z * 512 + core * 256 + from_x * 64, 64), 64)
        return kvbuf.at[item, rows, pl.ds(kind * HDIM, HDIM)]

    def kv_spread(item):
        for kind in kinds(item):
            for at, dx in enumerate((2, 1, 3)):
                to_x = shifted(x, dx)
                copy = remote(
                    kv_source(item, kind, to_x),
                    kv_landing(item, kind, x),
                    a_send.at[item, kind, at],
                    a_recv.at[item, kind, at],
                    device_at(y, to_x, z, core),
                )
                copy.start()
                waits_at_end.append(copy)
            pltpu.make_async_copy(
                kv_source(item, kind, x), kv_landing(item, kind, x), a_local.at[item, kind]
            ).start()

    def kv_block(item, from_z, from_core, part):
        start, count = ((0, 4), (0, 2), (2, 2))[part]
        if item == META:
            return metabuf.at[pl.ds(from_z * 8 + from_core * 4 + start, count)]
        rows = pl.ds(
            pl.multiple_of(from_z * 512 + from_core * 256 + start * 64, 64), count * 64
        )
        return kvbuf.at[item, rows]

    z_up, z_down, z_far = shifted(z, 1), shifted(z, 3), shifted(z, 2)
    up, down = device_at(y, x, z_up, core), device_at(y, x, z_down, core)

    def push(ref, sends, recvs, item, at, peer, came=None):
        copy = remote(ref, ref, sends.at[item, at], recvs.at[item, at if came is None else came], peer)
        copy.start()
        return copy

    def arrived(ref, sends, recvs, item, at, peer):
        remote(ref, ref, sends.at[item, at], recvs.at[item, at], peer).wait_recv()

    def kv_own(item):
        for kind in kinds(item):
            pltpu.make_async_copy(
                kv_source(item, kind, x), kv_landing(item, kind, x), a_local.at[item, kind]
            ).wait()
            for at, dx in enumerate((2, 1, 3)):
                landed = kv_landing(item, kind, shifted(x, -dx))
                remote(
                    landed, landed, a_send.at[item, kind, at], a_recv.at[item, kind, at], sibling
                ).wait_recv()
        block = kv_block(item, z, core, 0)
        waits_at_end.append(push(block, b_send, b_recv, item, 0, up))
        waits_at_end.append(push(block, b_send, b_recv, item, 1, down))
        waits_at_end.append(push(block, c_send, c_recv, item, 0, sibling))

    def kv_forward(item):
        block = kv_block(item, z_down, core, 0)
        arrived(block, b_send, b_recv, item, 0, up)
        waits_at_end.append(push(kv_block(item, z_down, core, 1), b_send, b_recv, item, 2, up))
        waits_at_end.append(push(block, c_send, c_recv, item, 1, sibling))
        block = kv_block(item, z_up, core, 0)
        arrived(block, b_send, b_recv, item, 1, down)
        waits_at_end.append(push(kv_block(item, z_up, core, 2), b_send, b_recv, item, 3, down))
        waits_at_end.append(push(block, c_send, c_recv, item, 2, sibling))

    def kv_far(item):
        for part in (1, 2):
            block = kv_block(item, z_far, core, part)
            arrived(block, b_send, b_recv, item, part + 1, up)
            waits_at_end.append(push(block, c_send, c_recv, item, part + 2, sibling))

    def kv_ready(item):
        for at, (from_z, part) in enumerate(
            ((z, 0), (z_down, 0), (z_up, 0), (z_far, 1), (z_far, 2))
        ):
            arrived(kv_block(item, from_z, 1 - core, part), c_send, c_recv, item, at, sibling)

    own_j = jnp.where(is_self, 1 - y, y - 2)

    def q_source(item, to_x):
        if item == META:
            return begin_ref
        return queries.at[:, pl.ds(pl.multiple_of(to_x * GROUP + item * HDIM, HDIM), HDIM)]

    def q_landing(item, from_x):
        if item == META:
            return beginbuf.at[own_j * 4 + from_x]
        rows = pl.ds(pl.multiple_of(own_j * 512 + from_x * TOKENS, TOKENS), TOKENS)
        return qbuf.at[item, rows]

    def q_own_copy(item):
        return pltpu.make_async_copy(q_source(item, x), q_landing(item, x), qa_local.at[item])

    def q_spread_copies(item):
        return [
            remote(
                q_source(item, shifted(x, dx)),
                q_landing(item, x),
                qa_send.at[item, at],
                qa_recv.at[item, at],
                device_at(y, shifted(x, dx), z, core),
            )
            for at, dx in enumerate((2, 1, 3))
        ]

    def q_spread(item):
        for copy in q_spread_copies(item):
            copy.start()
        q_own_copy(item).start()

    def q_block(item, j):
        if item == META:
            return beginbuf.at[pl.ds(j * 4, 4)]
        return qbuf.at[item, pl.ds(pl.multiple_of(j * 512, 512), 512)]

    def q_push(item, at):
        peer = (other, partner, other)[at]
        return remote(
            q_block(item, own_j),
            q_block(item, own_j),
            qb_send.at[item, at],
            qb_recv.at[item, (0, 0, 1)[at]],
            peer,
        )

    def q_own(item):
        q_own_copy(item).wait()
        for at, dx in enumerate((2, 1, 3)):
            arrived(q_landing(item, shifted(x, -dx)), qa_send, qa_recv, item, at, sibling)
        q_push(item, 1).start()
        q_push(item, 0).start()

    def q_relay(item):
        arrived(q_block(item, own_j), qb_send, qb_recv, item, 0, partner)
        q_push(item, 2).start()

    def q_pass(item):
        @pl.when(is_cross)
        def _():
            q_own(item)

        @pl.when(is_self)
        def _():
            q_relay(item)

    def q_ready(item):
        @pl.when(is_cross)
        def _():
            arrived(q_block(item, 1 - own_j), qb_send, qb_recv, item, 0, other)

        @pl.when(is_self)
        def _():
            arrived(q_block(item, 1 - own_j), qb_send, qb_recv, item, 1, other)

    lanes = lax.broadcasted_iota(jnp.int32, (128, 128), 1)
    sublanes = lax.broadcasted_iota(jnp.int32, (128, 128), 0)
    causal = sublanes >= lanes
    diagonal = sublanes == lanes

    def inverse_rms(values):
        return lax.rsqrt(jnp.mean(values * values, axis=1, keepdims=True) + EPSILON)

    def decay_column(head):
        return jnp.sum(jnp.where(lanes == head, decays[...], 0.0), axis=1, keepdims=True)

    def decay_setup():
        decays[...] = jnp.ones((128, 128), jnp.float32)
        decays_t[...] = jnp.ones((128, 128), jnp.float32)
        for head in range(HEADS):
            decays[head : head + 1, :] = gates_ref[head]
            picked = table_ref[rate_ref[0, head]]
            decays_t[head : head + 1, :] = jnp.full((1, 128), picked, jnp.float32)
        turned = jnp.dot(
            jnp.log(decays_t[...]) + jnp.log(decays[...]),
            jnp.where(sublanes <= lanes, 1.0, 0.0),
            precision=lax.Precision.HIGHEST,
            preferred_element_type=jnp.float32,
        )
        decays_t[...] = turned
        decays[...] = jnp.transpose(turned)
        fade_out[...] = jnp.broadcast_to(jnp.exp(turned[:, 127:128])[0:24], (24, 128))

    def retain(first, last):
        scale = inverse_rms(x_ref[...].astype(jnp.float32))

        def one(head, carry):
            columns = pl.ds(pl.multiple_of(head * HDIM, HDIM), HDIM)
            values = x_ref[:, columns]
            normed = values.astype(jnp.float32) * scale
            query = (normed * query_gain_ref[:, columns]).astype(jnp.bfloat16)
            key_rows = (normed * key_gain_ref[:, columns]).astype(jnp.bfloat16)
            queries[:, columns] = query
            products = lax.dot_general(
                query, key_rows, (((1,), (1,)), ((), ())), preferred_element_type=jnp.float32
            )
            column = decay_column(head)
            row = decays_t[pl.ds(head, 1), :]
            weights = jnp.where(
                causal, products * jnp.exp(jnp.where(causal, column - row, 0.0)), 0.0
            ).astype(jnp.bfloat16)
            inside[:, columns] = jnp.dot(weights, values, preferred_element_type=jnp.float32)
            fading = jnp.exp(row[:, 127:128] - column)
            faded = (key_rows.astype(jnp.float32) * fading).astype(jnp.bfloat16)
            update_out[pl.ds(head, 1)] = lax.dot_general(
                faded, values, (((0,), (0,)), ((), ())), preferred_element_type=jnp.float32
            ).astype(jnp.bfloat16)[None]
            return carry

        lax.fori_loop(first, last, one, 0)

    def update_copies():
        copies = []
        for at in range(8):
            to_seq, peer = seq_peer(at)
            rows = pl.ds(pl.multiple_of(to_seq * 16, 16), 16)
            pairs = (
                (update_out.at[:, rows, :], update_in.at[seq]),
                (fade_out, fade_in.at[seq]),
            )
            for kind, (src, dst) in enumerate(pairs):
                if at == 0:
                    copies.append(pltpu.make_async_copy(src, dst, s_local.at[1 + kind]))
                else:
                    copies.append(
                        remote(src, dst, u_send.at[at, kind], u_recv.at[at, kind], peer)
                    )
        return copies

    def enter_copies():
        copies = []
        for at in range(8):
            to_seq, peer = seq_peer(at)
            dst = enter_in.at[:, pl.ds(pl.multiple_of(seq * 16, 16), 16), :]
            if at == 0:
                copies.append(pltpu.make_async_copy(enter_out.at[to_seq], dst, s_local.at[3]))
            else:
                copies.append(
                    remote(enter_out.at[to_seq], dst, e_send.at[at], e_recv.at[at], peer)
                )
        return copies

    def scan():
        def one(head, carry):
            now = kept[pl.ds(head, 1)][0]
            for at in range(8):
                enter_out[at, pl.ds(head, 1)] = now.astype(jnp.bfloat16)[None]
                fade = fade_in[at, pl.ds(head, 1), :]
                now = fade * now + update_in[at, pl.ds(head, 1)][0].astype(jnp.float32)
            state_out[pl.ds(head, 1)] = now[None]
            return carry

        lax.fori_loop(0, HEADS, one, 0)

    def mix(first, last):
        def one(head, carry):
            columns = pl.ds(pl.multiple_of(head * HDIM, HDIM), HDIM)
            carried = jnp.dot(
                queries[:, columns], enter_in[pl.ds(head, 1)][0], preferred_element_type=jnp.float32
            )
            retained = inside[:, columns] + jnp.exp(decay_column(head)) * carried
            mixed = retained * inverse_rms(retained)
            result[:, columns] = (
                x_ref[:, columns].astype(jnp.float32) + mixed * out_gain_ref[:, columns]
            ).astype(jnp.bfloat16)
            return carry

        lax.fori_loop(first, last, one, 0)

    def self_result(group):
        columns = pl.ds(group * GROUP, GROUP)
        return remote(
            result.at[:, columns], out_ref.at[:, columns], w_send.at[group], w_recv.at[group], after
        )

    def fresh_rows(to):
        return result.at[pl.ds(pl.multiple_of((to // 2) * 16, 16), 16)]

    own_fresh = pltpu.make_async_copy(fresh_rows(section), fresh, s_local.at[4])

    def fresh_copy(by):
        to = lax.rem(section + by, 16)
        return remote(fresh_rows(to), fresh, f_send.at[by], f_recv.at[0], (to, seq))

    first_j = 1 - own_j

    def place_setup():
        lane = lax.broadcasted_iota(jnp.int32, (1, 128), 1)
        for pair in range(16):
            pos_ref[:, pair * 128 : (pair + 1) * 128] = jnp.where(
                lane < 64,
                metabuf[2 * pair, 0:1, :],
                pltpu.roll(metabuf[2 * pair + 1, 0:1, :], 64, 1),
            )

    def attend(item, j):
        index = lax.broadcasted_iota(jnp.int32, (QBLOCK, 128), 0) + z * 256
        wide = lax.broadcasted_iota(jnp.int32, (QBLOCK, QBLOCK), 0) == (
            lax.broadcasted_iota(jnp.int32, (QBLOCK, QBLOCK), 1)
        )

        def block(at, carry):
            rows = pl.ds(pl.multiple_of(j * 512 + at * QBLOCK, QBLOCK), QBLOCK)
            query = qbuf[item, rows, :]
            places = index + beginbuf[j * 4 + at * 2][0:1, :]
            highest = jnp.full((QBLOCK, 128), MASKED_SCORE, jnp.float32)
            for chunk in range(KEYS // KCHUNK):
                keys = kvbuf[item, chunk * KCHUNK : (chunk + 1) * KCHUNK, 0:HDIM]
                scores = lax.dot_general(
                    query, keys, (((1,), (1,)), ((), ())), preferred_element_type=jnp.float32
                )
                for part in range(KCHUNK // 128):
                    here = slice(chunk * KCHUNK + part * 128, chunk * KCHUNK + (part + 1) * 128)
                    piece = jnp.where(
                        pos_ref[:, here] <= places,
                        scores[:, part * 128 : (part + 1) * 128],
                        MASKED_SCORE,
                    )
                    scores_ref[:, here] = piece
                    highest = jnp.maximum(highest, piece)
            top = jnp.max(highest, axis=1, keepdims=True)
            totals = jnp.zeros((QBLOCK, 128), jnp.float32)
            pieces = jnp.zeros((QBLOCK, HDIM), jnp.float32)
            for chunk in range(KEYS // KCHUNK):
                here = slice(chunk * KCHUNK, (chunk + 1) * KCHUNK)
                likely = jnp.exp2((scores_ref[:, here] - top) * STEP)
                for part in range(KCHUNK // 128):
                    totals += likely[:, part * 128 : (part + 1) * 128]
                pieces += jnp.dot(
                    likely.astype(jnp.bfloat16),
                    kvbuf[item, here, HDIM : 2 * HDIM],
                    preferred_element_type=jnp.float32,
                )
            total = jnp.sum(totals, axis=1, keepdims=True)
            o_out[item, rows, :] = (pieces / total).astype(jnp.bfloat16)
            lse = top * HDIM ** (-0.5) + jnp.log(total)
            flat = jnp.sum(jnp.where(wide, lse, 0.0), axis=0, keepdims=True)
            lse_out[item, j, pl.ds(at * 2, 1), :] = flat[:, 0:128]
            lse_out[item, j, pl.ds(at * 2 + 1, 1), :] = flat[:, 128:256]
            return carry

        lax.fori_loop(0, 2, block, 0)

    def pieces_of(item, j):
        return o_out.at[item, pl.ds(pl.multiple_of(j * 512, 512), 512)], lse_out.at[item, j]

    def piece_copies(item, at):
        peer, j = ((other, first_j), (partner, own_j))[at]
        o_src, lse_src = pieces_of(item, j)
        return [
            remote(o_src, o_in.at[item, at], o_send.at[item, at, 0], o_recv.at[item, at, 0], peer),
            remote(
                lse_src, lse_in.at[item, at], o_send.at[item, at, 1], o_recv.at[item, at, 1], peer
            ),
        ]

    def shares_of(tiles):
        overall = tiles[0]
        for tile in tiles[1:]:
            overall = jnp.maximum(overall, tile)
        shares = [jnp.exp(tile - overall) for tile in tiles]
        whole = shares[0]
        for share in shares[1:]:
            whole = whole + share
        return [share / whole for share in shares], overall + jnp.log(whole)

    def weighted(shares, parts, group):
        total = jnp.zeros((TOKENS, HDIM), jnp.float32)
        for share, part in zip(shares, parts):
            column = jnp.sum(
                jnp.where(diagonal, share[group : group + 1, :], 0.0), axis=1, keepdims=True
            )
            total += column * part.astype(jnp.float32)
        return total.astype(jnp.bfloat16)

    def own_rows(group):
        return pl.ds(pl.multiple_of(own_j * 512 + group * TOKENS, TOKENS), TOKENS)

    def merge_self(item):
        for copy in piece_copies(item, 0):
            copy.wait_recv()
        shares, lse = shares_of([lse_out[item, own_j], lse_in[item, 0]])
        for group in range(4):
            here = slice(group * TOKENS, (group + 1) * TOKENS)
            o_out[item, own_rows(group), :] = weighted(
                shares, (o_out[item, own_rows(group), :], o_in[item, 0, here, :]), group
            )
        lse_out[item, own_j] = lse
        for copy in piece_copies(item, 1):
            copy.start()

    def att_copies(item):
        copies = [
            pltpu.make_async_copy(
                att_out.at[item, pl.ds(pl.multiple_of(x * TOKENS, TOKENS), TOKENS)],
                att_in.at[item, x],
                t_local.at[item],
            )
        ]
        for at, dx in enumerate((2, 1, 3)):
            to_x = shifted(x, dx)
            copies.append(
                remote(
                    att_out.at[item, pl.ds(pl.multiple_of(to_x * TOKENS, TOKENS), TOKENS)],
                    att_in.at[item, x],
                    t_send.at[item, at],
                    t_recv.at[item, at],
                    device_at(y, to_x, z, core),
                )
            )
        return copies

    def merge_cross(item):
        for at in range(2):
            for copy in piece_copies(item, at):
                copy.wait_recv()
        shares, _ = shares_of([lse_out[item, own_j], lse_in[item, 0], lse_in[item, 1]])
        for group in range(4):
            here = slice(group * TOKENS, (group + 1) * TOKENS)
            att_out[item, here, :] = weighted(
                shares,
                (
                    o_out[item, own_rows(group), :],
                    o_in[item, 0, here, :],
                    o_in[item, 1, here, :],
                ),
                group,
            )
        for copy in att_copies(item):
            copy.start()

    def att_result(item, group):
        columns = pl.ds(group * GROUP + item * HDIM, HDIM)
        return remote(
            result.at[:, columns],
            out_ref.at[:, columns],
            r_send.at[item, group],
            r_recv.at[item, group],
            after,
        )

    def finish(item):
        for copy in att_copies(item):
            copy.wait()
        for group in range(4):
            here = slice(group * GROUP + item * HDIM, group * GROUP + (item + 1) * HDIM)
            result[:, here] = (
                x_ref[:, here].astype(jnp.float32)
                + att_in[item, group].astype(jnp.float32) * out_gain_ref[:, here]
            ).astype(jnp.bfloat16)
            att_result(item, group).start()

    for copy in fetches:
        copy.wait()
    meta_ref[0:1, 0:64] = positions_ref[...]
    begin_ref[...] = jnp.full((8, 128), start_ref[0, 0], jnp.int32)

    @pl.when(is_cross)
    def _():
        rows = x_ref[...].astype(jnp.float32)
        queries[...] = (rows * inverse_rms(rows) * query_gain_ref[...]).astype(jnp.bfloat16)

    @pl.when(is_self)
    def _():
        decay_setup()

    pl.semaphore_wait(barrier, len(peers) + 1 + jnp.where(is_root, 15, 0))

    for item in (META, 0, 1, 2, 3, 4):
        kv_spread(item)

        @pl.when(is_cross)
        def _():
            q_spread(item)

    kv_own(META)
    kv_own(0)
    kv_own(1)

    @pl.when(is_cross)
    def _():
        q_own(META)
        q_own(0)
        q_own(1)

    @pl.when(is_self)
    def _():
        retain(0, 7)
        q_relay(META)
        q_relay(0)

    kv_forward(META)
    kv_forward(0)
    kv_own(2)

    @pl.when(is_self)
    def _():
        retain(7, 14)
        q_relay(1)

    kv_far(META)
    kv_far(0)
    kv_forward(1)
    kv_own(3)

    @pl.when(is_self)
    def _():
        retain(14, HEADS)
        for copy in update_copies():
            copy.start()

    q_ready(META)
    kv_ready(META)
    place_setup()
    kv_far(1)
    kv_forward(2)
    kv_own(4)

    def service(step):
        if step == 0:
            q_pass(2)
        if step == 1:
            kv_far(2)
            kv_forward(3)
            q_pass(3)
        if step == 2:
            kv_far(3)
            kv_forward(4)
            q_pass(4)
        if step == 3:
            kv_far(4)

    for item in range(LOCAL_HEADS):
        q_ready(item)
        kv_ready(item)
        attend(item, first_j)
        for copy in piece_copies(item, 0):
            copy.start()
        service(item)
        attend(item, own_j)

        @pl.when(is_self)
        def _():
            merge_self(item)

        if item == 1:
            state_rows.wait()

            @pl.when(is_cross)
            def _():
                state_out[...] = kept[...]

            @pl.when(is_self)
            def _():
                for copy in update_copies():
                    copy.wait()
                scan()
                for copy in enter_copies():
                    copy.start()

        if item == 3:

            @pl.when(is_self)
            def _():
                for copy in enter_copies():
                    copy.wait()
                mix(0, HEADS)
                for group in range(4):
                    self_result(group).start()

            @pl.when(is_root)
            def _():
                own_fresh.start()
                for by in range(1, 16):
                    fresh_copy(by).start()

        @pl.when(is_cross)
        def _():
            if item >= 2:
                merge_cross(item - 2)
            if item >= 3:
                finish(item - 3)

    @pl.when(is_cross)
    def _():
        merge_cross(3)
        finish(2)
        merge_cross(4)
        finish(3)
        finish(4)

    @pl.when(is_root)
    def _():
        own_fresh.wait()

    @pl.when(jnp.logical_not(is_root))
    def _():
        fresh_copy(1).wait_recv()

    both = fresh[...].astype(jnp.float32)
    new_rows = jnp.where(core == 0, both[0:8], both[8:16])
    new_rows = new_rows * inverse_rms(new_rows)
    global_out[:, 0:HD] = (new_rows * global_ref[0:1, :]).astype(jnp.bfloat16)
    global_out[:, HD : 2 * HD] = (new_rows * global_ref[1:2, :]).astype(jnp.bfloat16)

    from_self = jnp.logical_and(section >= 1, section <= 8)

    @pl.when(from_self)
    def _():
        for group in range(4):
            self_result(group).wait_recv()

    @pl.when(jnp.logical_not(from_self))
    def _():
        for item in range(LOCAL_HEADS):
            for group in range(4):
                att_result(item, group).wait_recv()

    for copy in waits_at_end:
        copy.wait_send()
    for item in range(LOCAL_HEADS):
        for copy in piece_copies(item, 0):
            copy.wait_send()

    @pl.when(is_cross)
    def _():
        for item in range(LOCAL_HEADS + 1):
            for copy in q_spread_copies(item):
                copy.wait_send()
            q_push(item, 0).wait_send()
            q_push(item, 1).wait_send()
        for item in range(LOCAL_HEADS):
            for group in range(4):
                att_result(item, group).wait_send()

    @pl.when(is_self)
    def _():
        for item in range(LOCAL_HEADS + 1):
            q_push(item, 2).wait_send()
        for item in range(LOCAL_HEADS):
            for copy in piece_copies(item, 1):
                copy.wait_send()
        for group in range(4):
            self_result(group).wait_send()

    @pl.when(is_root)
    def _():
        for by in range(1, 16):
            fresh_copy(by).wait_send()


def span(*arguments):
    vmem = pl.BlockSpec(memory_space=pltpu.VMEM)
    hbm = pl.BlockSpec(memory_space=pl.ANY)
    dma = pltpu.SemaphoreType.DMA
    items = LOCAL_HEADS + 1

    def bf16(*shape):
        return pltpu.VMEM(shape, jnp.bfloat16)

    def f32(*shape):
        return pltpu.VMEM(shape, jnp.float32)

    def i32(*shape):
        return pltpu.VMEM(shape, jnp.int32)

    return pl.pallas_call(
        span_kernel,
        out_shape=(
            jax.ShapeDtypeStruct((TOKENS, HD), jnp.bfloat16),
            jax.ShapeDtypeStruct((HEADS, 16, HDIM), jnp.float32),
            jax.ShapeDtypeStruct((8, 2 * HD), jnp.bfloat16),
        ),
        in_specs=[hbm] * 12,
        out_specs=(vmem, vmem, vmem),
        scratch_shapes=[
            bf16(TOKENS, HD),
            pltpu.SMEM((16,), jnp.float32),
            pltpu.SMEM((1, 1), jnp.int32),
            pltpu.SMEM((1, HEADS), jnp.int32),
            f32(HEADS, 1, TOKENS),
            f32(1, HD),
            f32(1, HD),
            f32(1, HD),
            f32(2, HD),
            i32(1, 64),
            dma((10,)),
            bf16(TOKENS, HD),
            i32(8, 128),
            i32(8, 128),
            bf16(LOCAL_HEADS, KEYS, 2 * HDIM),
            i32(32, 8, 128),
            i32(8, 8, 128),
            bf16(LOCAL_HEADS, 1024, HDIM),
            f32(QBLOCK, KEYS),
            i32(1, KEYS),
            bf16(LOCAL_HEADS, 1024, HDIM),
            f32(LOCAL_HEADS, 2, 8, 128),
            bf16(LOCAL_HEADS, 2, 512, HDIM),
            f32(LOCAL_HEADS, 2, 8, 128),
            bf16(LOCAL_HEADS, 512, HDIM),
            bf16(LOCAL_HEADS, 4, TOKENS, HDIM),
            bf16(TOKENS, HD),
            f32(128, 128),
            f32(128, 128),
            f32(TOKENS, HD),
            f32(HEADS, 16, HDIM),
            bf16(HEADS, HDIM, HDIM),
            f32(24, 128),
            bf16(8, HEADS, 16, HDIM),
            f32(8, 24, 128),
            bf16(8, HEADS, 16, HDIM),
            bf16(HEADS, HDIM, HDIM),
            bf16(16, HD),
            dma((items, 2, 3)),
            dma((items, 2, 3)),
            dma((items, 2)),
            dma((items, 4)),
            dma((items, 4)),
            dma((items, 5)),
            dma((items, 5)),
            dma((items, 3)),
            dma((items, 3)),
            dma((items,)),
            dma((items, 3)),
            dma((items, 2)),
            dma((LOCAL_HEADS, 2, 2)),
            dma((LOCAL_HEADS, 2, 2)),
            dma((LOCAL_HEADS, 3)),
            dma((LOCAL_HEADS, 3)),
            dma((LOCAL_HEADS,)),
            dma((8, 2)),
            dma((8, 2)),
            dma((8,)),
            dma((8,)),
            dma((5,)),
            dma((LOCAL_HEADS, 4)),
            dma((LOCAL_HEADS, 4)),
            dma((4,)),
            dma((4,)),
            dma((16,)),
            dma((1,)),
        ],
        compiler_params=pltpu.CompilerParams(
            collective_id=0, has_side_effects=True, vmem_limit_bytes=58 * 1024 * 1024
        ),
        name="span",
    )(*arguments)


def local(
    section_input,
    state_in,
    decay_table,
    head_rate,
    gates,
    query_gain,
    key_gain,
    out_gain,
    global_gain,
    cache_kv,
    cache_pos,
    span_start,
):
    section_output, state_out, global_new = span(
        section_input[0],
        state_in[0],
        decay_table,
        head_rate,
        jnp.transpose(gates, (2, 0, 1)),
        query_gain,
        key_gain,
        out_gain,
        global_gain,
        cache_kv,
        cache_pos[None],
        span_start[None],
    )
    return (section_output[None], state_out[None], global_new[None, None])


def solution(mesh):
    return jax.shard_map(
        local,
        mesh=mesh,
        in_specs=(
            P("section", "seq", None),
            P("section", None, None, None),
            P(),
            P("section", None),
            P("section", "seq", None),
            P("section", None),
            P("section", None),
            P("section", None),
            P(),
            P(("section", "seq"), None),
            P(("section", "seq")),
            P("section"),
        ),
        out_specs=(
            P("section", "seq", None),
            P("section", None, "seq", None),
            P("seq", "section", None, None),
        ),
        check_vma=False,
    )
```

time: 108 us -> 94.5 us (0.88)
  the two profiles are of different devices: /device:TPU:17 before, /device:TPU:56 now
where the time goes in v3:
time: 94.5 us; the launch traced here: 94.3 us
  Pallas kernels  89.7 us (95%)
  local copies, waits for them, and re-layouts  3.32 us (4%)
  between operations  1.31 us (1%)
    pallas_call x1, Pallas kernels, span(): pl.pallas_call(span_kernel, out_shape=(jax.ShapeDtypeStruct((TOKENS, HD),...  89.7 us
    unnamed x7, local copies, waits for them, and re-layouts  3.32 us

profile of v3, /device:TPU:56, one launch (start us, length us, event | category | flops | bytes accessed | tf_op | source)
XLA Modules:
  0.0 94.3 jit_solution(9579638133596172761)
XLA Ops:
  1.3 89.7 %span.1 = (bf16[128,2560]{1,0:T(8,128)(2,1)}, f32[20,16,128]{2,1,0:T(8,128)}, bf16[8,5120]{1,0:T(8,128)(2,1)}) custom-call(bf16[128,2560]{1,0:T(8,128)(2,1)} %bitcast.11, f32[20,128,128]{2,1,0:T(8,128)} %bitcast.9, f32[16]{0:T(128)} %table_hbm.1, s32[1,20]{1,0:T(1,128)} %rate_hbm.1, f32[20,1,128]{2,1,0:T(1,128)} %bitcast.14, f32[1,2560]{1,0:T(1,128)} %query_gain_hbm.1, ...), custom_call_target="tpu_custom_call" | custom-call | tf_op jit(solution)/shard_map/span/pallas_call | solution.py:859
  91.0 0.0 copy-start
  91.0 0.0 copy-start.1
  91.0 2.0 %copy.19 = bf16[1,128,2560]{2,1,0:T(8,128)(2,1)} copy(bf16[1,128,2560]{2,1,0:T(8,128)(2,1)} %bitcast.10) | data formatting | bytes 1310720
  93.0 0.0 copy-done
  93.0 0.7 copy.20
  93.7 0.0 copy-done.1
  93.7 0.6 copy.21
Async XLA Ops:
  91.0 2.0 %copy-start = (f32[20,16,128]{2,1,0:T(8,128)S(1)}, f32[20,16,128]{2,1,0:T(8,128)}, u32[]{:S(2)}) copy-start(f32[20,16,128]{2,1,0:T(8,128)} %get-tuple-element.7) | copy-start | bytes 491524
  91.0 2.7 %copy-start.1 = (bf16[8,5120]{1,0:T(8,128)(2,1)S(1)}, bf16[8,5120]{1,0:T(8,128)(2,1)}, u32[]{:S(2)}) copy-start(bf16[8,5120]{1,0:T(8,128)(2,1)} %get-tuple-element.8) | copy-start | bytes 245764

commit v4 on v3

--- a/solution.py
+++ b/solution.py
@@ -74,7 +74,10 @@
     metabuf,
     beginbuf,
     qbuf,
-    scores_ref,
+    scores_even,
+    scores_odd,
+    top_even,
+    top_odd,
     pos_ref,
     o_out,
     lse_out,
@@ -165,7 +168,7 @@
         return to_z * 2 + to_x % 2, device_at(y, to_x, to_z, core)
 
     peers = [sibling, other, partner]
-    peers += [device_at(y, shifted(x, dx), z, core) for dx in (1, 2, 3)]
+    peers += [device_at(y, shifted(x, dx), z, core) for dx in (1, 3)]
     peers += [seq_peer(at)[1] for at in range(2, 8)]
     barrier = pltpu.get_barrier_semaphore()
     for peer in peers + [before]:
@@ -175,58 +178,58 @@
     def _():
         pl.semaphore_signal(barrier, inc=1, device_id=(7, seq), device_id_type=MESH)
 
-    waits_at_end = []
-
     META = LOCAL_HEADS
 
+    def is_meta(item):
+        return isinstance(item, int) and item == META
+
     def kinds(item):
-        return (0,) if item == META else (0, 1)
-
-    def kv_source(item, kind, to_x):
-        if item == META:
+        return (0,) if is_meta(item) else (0, 1)
+
+    def kv_source(item, kind, to_z):
+        if is_meta(item):
             return meta_ref
-        column = to_x * GROUP + item * HDIM + kind * HD
+        column = to_z * GROUP + item * HDIM + kind * HD
         return kv_ref.at[:, pl.ds(pl.multiple_of(column, HDIM), HDIM)]
 
-    def kv_landing(item, kind, from_x):
-        if item == META:
-            return metabuf.at[z * 8 + core * 4 + from_x]
-        rows = pl.ds(pl.multiple_of(z * 512 + core * 256 + from_x * 64, 64), 64)
+    def kv_landing(item, kind, from_z):
+        if is_meta(item):
+            return metabuf.at[x * 8 + core * 4 + from_z]
+        rows = pl.ds(pl.multiple_of(x * 512 + core * 256 + from_z * 64, 64), 64)
         return kvbuf.at[item, rows, pl.ds(kind * HDIM, HDIM)]
 
+    def kv_spread_copies(item):
+        return [
+            remote(
+                kv_source(item, kind, shifted(z, dz)),
+                kv_landing(item, kind, z),
+                a_send.at[item, kind, at],
+                a_recv.at[item, kind, at],
+                device_at(y, x, shifted(z, dz), core),
+            )
+            for kind in kinds(item)
+            for at, dz in enumerate((2, 1, 3))
+        ]
+
     def kv_spread(item):
+        for copy in kv_spread_copies(item):
+            copy.start()
         for kind in kinds(item):
-            for at, dx in enumerate((2, 1, 3)):
-                to_x = shifted(x, dx)
-                copy = remote(
-                    kv_source(item, kind, to_x),
-                    kv_landing(item, kind, x),
-                    a_send.at[item, kind, at],
-                    a_recv.at[item, kind, at],
-                    device_at(y, to_x, z, core),
-                )
-                copy.start()
-                waits_at_end.append(copy)
             pltpu.make_async_copy(
-                kv_source(item, kind, x), kv_landing(item, kind, x), a_local.at[item, kind]
+                kv_source(item, kind, z), kv_landing(item, kind, z), a_local.at[item, kind]
             ).start()
 
-    def kv_block(item, from_z, from_core, part):
+    def kv_block(item, from_x, from_core, part):
         start, count = ((0, 4), (0, 2), (2, 2))[part]
-        if item == META:
-            return metabuf.at[pl.ds(from_z * 8 + from_core * 4 + start, count)]
+        if is_meta(item):
+            return metabuf.at[pl.ds(from_x * 8 + from_core * 4 + start, count)]
         rows = pl.ds(
-            pl.multiple_of(from_z * 512 + from_core * 256 + start * 64, 64), count * 64
+            pl.multiple_of(from_x * 512 + from_core * 256 + start * 64, 64), count * 64
         )
         return kvbuf.at[item, rows]
 
-    z_up, z_down, z_far = shifted(z, 1), shifted(z, 3), shifted(z, 2)
-    up, down = device_at(y, x, z_up, core), device_at(y, x, z_down, core)
-
-    def push(ref, sends, recvs, item, at, peer, came=None):
-        copy = remote(ref, ref, sends.at[item, at], recvs.at[item, at if came is None else came], peer)
-        copy.start()
-        return copy
+    x_up, x_down, x_far = shifted(x, 1), shifted(x, 3), shifted(x, 2)
+    up, down = device_at(y, x_up, z, core), device_at(y, x_down, z, core)
 
     def arrived(ref, sends, recvs, item, at, peer):
         remote(ref, ref, sends.at[item, at], recvs.at[item, at], peer).wait_recv()
@@ -234,66 +237,85 @@
     def kv_own(item):
         for kind in kinds(item):
             pltpu.make_async_copy(
-                kv_source(item, kind, x), kv_landing(item, kind, x), a_local.at[item, kind]
+                kv_source(item, kind, z), kv_landing(item, kind, z), a_local.at[item, kind]
             ).wait()
-            for at, dx in enumerate((2, 1, 3)):
-                landed = kv_landing(item, kind, shifted(x, -dx))
+            for at, dz in enumerate((2, 1, 3)):
+                landed = kv_landing(item, kind, shifted(z, -dz))
                 remote(
                     landed, landed, a_send.at[item, kind, at], a_recv.at[item, kind, at], sibling
                 ).wait_recv()
-        block = kv_block(item, z, core, 0)
-        waits_at_end.append(push(block, b_send, b_recv, item, 0, up))
-        waits_at_end.append(push(block, b_send, b_recv, item, 1, down))
-        waits_at_end.append(push(block, c_send, c_recv, item, 0, sibling))
+        for copy in kv_pushes(item)[0:3]:
+            copy.start()
+
+    def kv_pushes(item):
+        here, below = kv_block(item, x, core, 0), kv_block(item, x_down, core, 0)
+        above = kv_block(item, x_up, core, 0)
+
+        def along(ref, at, peer):
+            return remote(ref, ref, b_send.at[item, at], b_recv.at[item, at], peer)
+
+        def across(ref, at):
+            return remote(ref, ref, c_send.at[item, at], c_recv.at[item, at], sibling)
+
+        return [
+            along(here, 0, up),
+            along(here, 1, down),
+            across(here, 0),
+            along(kv_block(item, x_down, core, 1), 2, up),
+            across(below, 1),
+            along(kv_block(item, x_up, core, 2), 3, down),
+            across(above, 2),
+            across(kv_block(item, x_far, core, 1), 3),
+            across(kv_block(item, x_far, core, 2), 4),
+        ]
 
     def kv_forward(item):
-        block = kv_block(item, z_down, core, 0)
-        arrived(block, b_send, b_recv, item, 0, up)
-        waits_at_end.append(push(kv_block(item, z_down, core, 1), b_send, b_recv, item, 2, up))
-        waits_at_end.append(push(block, c_send, c_recv, item, 1, sibling))
-        block = kv_block(item, z_up, core, 0)
-        arrived(block, b_send, b_recv, item, 1, down)
-        waits_at_end.append(push(kv_block(item, z_up, core, 2), b_send, b_recv, item, 3, down))
-        waits_at_end.append(push(block, c_send, c_recv, item, 2, sibling))
+        pushes = kv_pushes(item)
+        arrived(kv_block(item, x_down, core, 0), b_send, b_recv, item, 0, up)
+        pushes[3].start()
+        pushes[4].start()
+        arrived(kv_block(item, x_up, core, 0), b_send, b_recv, item, 1, down)
+        pushes[5].start()
+        pushes[6].start()
 
     def kv_far(item):
+        pushes = kv_pushes(item)
         for part in (1, 2):
-            block = kv_block(item, z_far, core, part)
-            arrived(block, b_send, b_recv, item, part + 1, up)
-            waits_at_end.append(push(block, c_send, c_recv, item, part + 2, sibling))
+            arrived(kv_block(item, x_far, core, part), b_send, b_recv, item, part + 1, up)
+            pushes[part + 6].start()
 
     def kv_ready(item):
-        for at, (from_z, part) in enumerate(
-            ((z, 0), (z_down, 0), (z_up, 0), (z_far, 1), (z_far, 2))
+        for at, (from_x, part) in enumerate(
+            ((x, 0), (x_down, 0), (x_up, 0), (x_far, 1), (x_far, 2))
         ):
-            arrived(kv_block(item, from_z, 1 - core, part), c_send, c_recv, item, at, sibling)
+            arrived(kv_block(item, from_x, 1 - core, part), c_send, c_recv, item, at, sibling)
 
     own_j = jnp.where(is_self, 1 - y, y - 2)
 
-    def q_source(item, to_x):
-        if item == META:
+    def q_source(item, to_z):
+        if is_meta(item):
             return begin_ref
-        return queries.at[:, pl.ds(pl.multiple_of(to_x * GROUP + item * HDIM, HDIM), HDIM)]
-
-    def q_landing(item, from_x):
-        if item == META:
-            return beginbuf.at[own_j * 4 + from_x]
-        rows = pl.ds(pl.multiple_of(own_j * 512 + from_x * TOKENS, TOKENS), TOKENS)
+        return queries.at[:, pl.ds(pl.multiple_of(to_z * GROUP + item * HDIM, HDIM), HDIM)]
+
+    def q_landing(item, from_z):
+        if is_meta(item):
+            return beginbuf.at[own_j * 4 + from_z]
+        rows = pl.ds(pl.multiple_of(own_j * 512 + from_z * TOKENS, TOKENS), TOKENS)
         return qbuf.at[item, rows]
 
     def q_own_copy(item):
-        return pltpu.make_async_copy(q_source(item, x), q_landing(item, x), qa_local.at[item])
+        return pltpu.make_async_copy(q_source(item, z), q_landing(item, z), qa_local.at[item])
 
     def q_spread_copies(item):
         return [
             remote(
-                q_source(item, shifted(x, dx)),
-                q_landing(item, x),
+                q_source(item, shifted(z, dz)),
+                q_landing(item, z),
                 qa_send.at[item, at],
                 qa_recv.at[item, at],
-                device_at(y, shifted(x, dx), z, core),
-            )
-            for at, dx in enumerate((2, 1, 3))
+                device_at(y, x, shifted(z, dz), core),
+            )
+            for at, dz in enumerate((2, 1, 3))
         ]
 
     def q_spread(item):
@@ -302,7 +324,7 @@
         q_own_copy(item).start()
 
     def q_block(item, j):
-        if item == META:
+        if is_meta(item):
             return beginbuf.at[pl.ds(j * 4, 4)]
         return qbuf.at[item, pl.ds(pl.multiple_of(j * 512, 512), 512)]
 
@@ -318,23 +340,14 @@
 
     def q_own(item):
         q_own_copy(item).wait()
-        for at, dx in enumerate((2, 1, 3)):
-            arrived(q_landing(item, shifted(x, -dx)), qa_send, qa_recv, item, at, sibling)
+        for at, dz in enumerate((2, 1, 3)):
+            arrived(q_landing(item, shifted(z, -dz)), qa_send, qa_recv, item, at, sibling)
         q_push(item, 1).start()
         q_push(item, 0).start()
 
     def q_relay(item):
         arrived(q_block(item, own_j), qb_send, qb_recv, item, 0, partner)
         q_push(item, 2).start()
-
-    def q_pass(item):
-        @pl.when(is_cross)
-        def _():
-            q_own(item)
-
-        @pl.when(is_self)
-        def _():
-            q_relay(item)
 
     def q_ready(item):
         @pl.when(is_cross)
@@ -399,7 +412,7 @@
             ).astype(jnp.bfloat16)[None]
             return carry
 
-        lax.fori_loop(first, last, one, 0)
+        lax.fori_loop(first, last, one, 0, unroll=4 if (last - first) % 4 == 0 else 5)
 
     def update_copies():
         copies = []
@@ -457,7 +470,7 @@
             ).astype(jnp.bfloat16)
             return carry
 
-        lax.fori_loop(first, last, one, 0)
+        lax.fori_loop(first, last, one, 0, unroll=4 if (last - first) % 4 == 0 else 5)
 
     def self_result(group):
         columns = pl.ds(group * GROUP, GROUP)
@@ -485,53 +498,82 @@
                 pltpu.roll(metabuf[2 * pair + 1, 0:1, :], 64, 1),
             )
 
-    def attend(item, j):
-        index = lax.broadcasted_iota(jnp.int32, (QBLOCK, 128), 0) + z * 256
-        wide = lax.broadcasted_iota(jnp.int32, (QBLOCK, QBLOCK), 0) == (
-            lax.broadcasted_iota(jnp.int32, (QBLOCK, QBLOCK), 1)
-        )
-
-        def block(at, carry):
-            rows = pl.ds(pl.multiple_of(j * 512 + at * QBLOCK, QBLOCK), QBLOCK)
-            query = qbuf[item, rows, :]
-            places = index + beginbuf[j * 4 + at * 2][0:1, :]
+    def tree(combine, values):
+        while len(values) > 1:
+            values = [
+                combine(values[at], values[at + 1]) if at + 1 < len(values) else values[at]
+                for at in range(0, len(values), 2)
+            ]
+        return values[0]
+
+    def block_of(step):
+        item, block = step // 4, step % 4
+        return item, jnp.where(block < 2, first_j, own_j), block % 2
+
+    def block_rows(j, at):
+        return pl.ds(pl.multiple_of(j * 512 + at * QBLOCK, QBLOCK), QBLOCK)
+
+    def stage(current, previous, even):
+        fill, fill_top = (scores_even, top_even) if even else (scores_odd, top_odd)
+        drain, drain_top = (scores_odd, top_odd) if even else (scores_even, top_even)
+        if current is not None:
+            item, j, at = block_of(current)
+            row = lax.broadcasted_iota(jnp.int32, (QBLOCK, 128), 0)
+            index = (at * 2 + row // TOKENS) * 256 + (x % 2) * TOKENS + row % TOKENS
+            query = qbuf[item, block_rows(j, at), :]
+            places = index + beginbuf[j * 4][0:1, :]
             highest = jnp.full((QBLOCK, 128), MASKED_SCORE, jnp.float32)
-            for chunk in range(KEYS // KCHUNK):
-                keys = kvbuf[item, chunk * KCHUNK : (chunk + 1) * KCHUNK, 0:HDIM]
+        if previous is not None:
+            item_p, j_p, at_p = block_of(previous)
+            top = drain_top[...][:, 0:1]
+            totals = jnp.zeros((QBLOCK, 128), jnp.float32)
+            pieces = jnp.zeros((QBLOCK, HDIM), jnp.float32)
+        for chunk in range(KEYS // KCHUNK):
+            here = slice(chunk * KCHUNK, (chunk + 1) * KCHUNK)
+            parts = [
+                slice(chunk * KCHUNK + part * 128, chunk * KCHUNK + (part + 1) * 128)
+                for part in range(KCHUNK // 128)
+            ]
+            if current is not None:
                 scores = lax.dot_general(
-                    query, keys, (((1,), (1,)), ((), ())), preferred_element_type=jnp.float32
+                    query,
+                    kvbuf[item, here, 0:HDIM],
+                    (((1,), (1,)), ((), ())),
+                    preferred_element_type=jnp.float32,
                 )
-                for part in range(KCHUNK // 128):
-                    here = slice(chunk * KCHUNK + part * 128, chunk * KCHUNK + (part + 1) * 128)
+            if previous is not None:
+                likely = [jnp.exp2((drain[:, part] - top) * STEP) for part in parts]
+                totals += tree(jnp.add, likely)
+                pieces += jnp.dot(
+                    jnp.concatenate([value.astype(jnp.bfloat16) for value in likely], axis=1),
+                    kvbuf[item_p, here, HDIM : 2 * HDIM],
+                    preferred_element_type=jnp.float32,
+                )
+            if current is not None:
+                masked = []
+                for at_part, part in enumerate(parts):
                     piece = jnp.where(
-                        pos_ref[:, here] <= places,
-                        scores[:, part * 128 : (part + 1) * 128],
+                        pos_ref[:, part] <= places,
+                        scores[:, at_part * 128 : (at_part + 1) * 128],
                         MASKED_SCORE,
                     )
-                    scores_ref[:, here] = piece
-                    highest = jnp.maximum(highest, piece)
-            top = jnp.max(highest, axis=1, keepdims=True)
-            totals = jnp.zeros((QBLOCK, 128), jnp.float32)
-            pieces = jnp.zeros((QBLOCK, HDIM), jnp.float32)
-            for chunk in range(KEYS // KCHUNK):
-                here = slice(chunk * KCHUNK, (chunk + 1) * KCHUNK)
-                likely = jnp.exp2((scores_ref[:, here] - top) * STEP)
-                for part in range(KCHUNK // 128):
-                    totals += likely[:, part * 128 : (part + 1) * 128]
-                pieces += jnp.dot(
-                    likely.astype(jnp.bfloat16),
-                    kvbuf[item, here, HDIM : 2 * HDIM],
-                    preferred_element_type=jnp.float32,
-                )
+                    fill[:, part] = piece
+                    masked.append(piece)
+                highest = jnp.maximum(highest, tree(jnp.maximum, masked))
+        if current is not None:
+            fill_top[...] = jnp.broadcast_to(
+                jnp.max(highest, axis=1, keepdims=True), (QBLOCK, 128)
+            )
+        if previous is not None:
             total = jnp.sum(totals, axis=1, keepdims=True)
-            o_out[item, rows, :] = (pieces / total).astype(jnp.bfloat16)
+            o_out[item_p, block_rows(j_p, at_p), :] = (pieces / total).astype(jnp.bfloat16)
             lse = top * HDIM ** (-0.5) + jnp.log(total)
+            wide = lax.broadcasted_iota(jnp.int32, (QBLOCK, QBLOCK), 0) == (
+                lax.broadcasted_iota(jnp.int32, (QBLOCK, QBLOCK), 1)
+            )
             flat = jnp.sum(jnp.where(wide, lse, 0.0), axis=0, keepdims=True)
-            lse_out[item, j, pl.ds(at * 2, 1), :] = flat[:, 0:128]
-            lse_out[item, j, pl.ds(at * 2 + 1, 1), :] = flat[:, 128:256]
-            return carry
-
-        lax.fori_loop(0, 2, block, 0)
+            lse_out[item_p, j_p, pl.ds(at_p * 2, 1), :] = flat[:, 0:128]
+            lse_out[item_p, j_p, pl.ds(at_p * 2 + 1, 1), :] = flat[:, 128:256]
 
     def pieces_of(item, j):
         return o_out.at[item, pl.ds(pl.multiple_of(j * 512, 512), 512)], lse_out.at[item, j]
@@ -584,20 +626,20 @@
     def att_copies(item):
         copies = [
             pltpu.make_async_copy(
-                att_out.at[item, pl.ds(pl.multiple_of(x * TOKENS, TOKENS), TOKENS)],
-                att_in.at[item, x],
+                att_out.at[item, pl.ds(pl.multiple_of(z * TOKENS, TOKENS), TOKENS)],
+                att_in.at[item, z],
                 t_local.at[item],
             )
         ]
-        for at, dx in enumerate((2, 1, 3)):
-            to_x = shifted(x, dx)
+        for at, dz in enumerate((2, 1, 3)):
+            to_z = shifted(z, dz)
             copies.append(
                 remote(
-                    att_out.at[item, pl.ds(pl.multiple_of(to_x * TOKENS, TOKENS), TOKENS)],
-                    att_in.at[item, x],
+                    att_out.at[item, pl.ds(pl.multiple_of(to_z * TOKENS, TOKENS), TOKENS)],
+                    att_in.at[item, z],
                     t_send.at[item, at],
                     t_recv.at[item, at],
-                    device_at(y, to_x, z, core),
+                    device_at(y, x, to_z, core),
                 )
             )
         return copies
@@ -621,8 +663,11 @@
         for copy in att_copies(item):
             copy.start()
 
+    def head_columns(item, group):
+        return pl.ds(pl.multiple_of(group * GROUP + item * HDIM, HDIM), HDIM)
+
     def att_result(item, group):
-        columns = pl.ds(group * GROUP + item * HDIM, HDIM)
+        columns = head_columns(item, group)
         return remote(
             result.at[:, columns],
             out_ref.at[:, columns],
@@ -635,151 +680,171 @@
         for copy in att_copies(item):
             copy.wait()
         for group in range(4):
-            here = slice(group * GROUP + item * HDIM, group * GROUP + (item + 1) * HDIM)
+            here = head_columns(item, group)
             result[:, here] = (
                 x_ref[:, here].astype(jnp.float32)
                 + att_in[item, group].astype(jnp.float32) * out_gain_ref[:, here]
             ).astype(jnp.bfloat16)
             att_result(item, group).start()
 
+    pl.semaphore_wait(barrier, len(peers) + 1 + jnp.where(is_root, 15, 0))
+    kv_spread(0)
     for copy in fetches:
         copy.wait()
     meta_ref[0:1, 0:64] = positions_ref[...]
     begin_ref[...] = jnp.full((8, 128), start_ref[0, 0], jnp.int32)
-
-    @pl.when(is_cross)
-    def _():
+    kv_spread(META)
+
+    def on_self(*steps):
+        @pl.when(is_self)
+        def _():
+            for step in steps:
+                step()
+
+    def on_cross(*steps):
+        @pl.when(is_cross)
+        def _():
+            for step in steps:
+                step()
+
+    def send_updates():
+        for copy in update_copies():
+            copy.start()
+
+    def enter():
+        for copy in update_copies():
+            copy.wait()
+        scan()
+        for copy in enter_copies():
+            copy.start()
+
+    def keep_state():
+        state_rows.wait()
+        on_cross(lambda: state_out.__setitem__(Ellipsis, kept[...]))
+        on_self(enter)
+
+    def self_mix():
+        for copy in enter_copies():
+            copy.wait()
+        for group in range(4):
+            mix(group * LOCAL_HEADS, (group + 1) * LOCAL_HEADS)
+            self_result(group).start()
+
+    def send_fresh():
+        @pl.when(is_root)
+        def _():
+            own_fresh.start()
+            for by in range(1, 16):
+                fresh_copy(by).start()
+
+    def own(item):
+        kv_own(item)
+        on_cross(lambda: q_own(item))
+
+    def make_queries():
         rows = x_ref[...].astype(jnp.float32)
         queries[...] = (rows * inverse_rms(rows) * query_gain_ref[...]).astype(jnp.bfloat16)
-
-    @pl.when(is_self)
-    def _():
-        decay_setup()
-
-    pl.semaphore_wait(barrier, len(peers) + 1 + jnp.where(is_root, 15, 0))
-
-    for item in (META, 0, 1, 2, 3, 4):
+        q_spread(META)
+        q_spread(0)
+
+    def spread(item):
         kv_spread(item)
-
-        @pl.when(is_cross)
-        def _():
-            q_spread(item)
-
-    kv_own(META)
-    kv_own(0)
-    kv_own(1)
-
-    @pl.when(is_cross)
-    def _():
-        q_own(META)
-        q_own(0)
-        q_own(1)
-
-    @pl.when(is_self)
-    def _():
-        retain(0, 7)
-        q_relay(META)
-        q_relay(0)
-
+        on_cross(lambda: q_spread(item))
+
+    on_cross(make_queries)
+    spread(1)
+    on_self(decay_setup, lambda: retain(0, 8))
+    own(META)
+    own(0)
+    spread(2)
+    on_self(lambda: retain(8, 16))
+    own(1)
+    spread(3)
     kv_forward(META)
     kv_forward(0)
-    kv_own(2)
-
-    @pl.when(is_self)
-    def _():
-        retain(7, 14)
-        q_relay(1)
-
+    on_self(lambda: retain(16, HEADS))
+    own(2)
+    spread(4)
+    on_self(lambda: q_relay(META), lambda: q_relay(0))
+    kv_forward(1)
     kv_far(META)
     kv_far(0)
-    kv_forward(1)
-    kv_own(3)
-
-    @pl.when(is_self)
-    def _():
-        retain(14, HEADS)
-        for copy in update_copies():
-            copy.start()
-
+    own(3)
+    on_self(lambda: q_relay(1))
+    kv_forward(2)
+    kv_far(1)
     q_ready(META)
     kv_ready(META)
     place_setup()
-    kv_far(1)
-    kv_forward(2)
-    kv_own(4)
-
-    def service(step):
-        if step == 0:
-            q_pass(2)
-        if step == 1:
-            kv_far(2)
-            kv_forward(3)
-            q_pass(3)
-        if step == 2:
-            kv_far(3)
-            kv_forward(4)
-            q_pass(4)
-        if step == 3:
-            kv_far(4)
-
-    for item in range(LOCAL_HEADS):
-        q_ready(item)
-        kv_ready(item)
-        attend(item, first_j)
-        for copy in piece_copies(item, 0):
-            copy.start()
-        service(item)
-        attend(item, own_j)
-
-        @pl.when(is_self)
+
+    hooks = {
+        15: (keep_state,),
+        0: (lambda: own(4), lambda: on_self(lambda: q_relay(2))),
+        1: (lambda: kv_forward(3),),
+        2: (lambda: kv_far(2),),
+        3: (lambda: on_self(lambda: q_relay(3)),),
+        4: (lambda: kv_forward(4),),
+        5: (lambda: kv_far(3),),
+        7: (lambda: on_self(lambda: q_relay(4)),),
+        8: (lambda: kv_far(4), lambda: on_self(send_updates)),
+        12: (lambda: on_cross(lambda: merge_cross(0)),),
+        16: (lambda: on_cross(lambda: finish(0), lambda: merge_cross(1)),),
+    }
+
+    def after_block(step):
+        item, block = step // 4, step % 4
+
+        @pl.when(block == 1)
         def _():
-            merge_self(item)
-
-        if item == 1:
-            state_rows.wait()
-
-            @pl.when(is_cross)
+            for copy in piece_copies(item, 0):
+                copy.start()
+
+        for due, steps in hooks.items():
+
+            @pl.when(step == due)
             def _():
-                state_out[...] = kept[...]
-
-            @pl.when(is_self)
-            def _():
-                for copy in update_copies():
-                    copy.wait()
-                scan()
-                for copy in enter_copies():
-                    copy.start()
-
-        if item == 3:
-
-            @pl.when(is_self)
-            def _():
-                for copy in enter_copies():
-                    copy.wait()
-                mix(0, HEADS)
-                for group in range(4):
-                    self_result(group).start()
-
-            @pl.when(is_root)
-            def _():
-                own_fresh.start()
-                for by in range(1, 16):
-                    fresh_copy(by).start()
-
-        @pl.when(is_cross)
+                for one in steps:
+                    one()
+
+        @pl.when(jnp.logical_and(is_self, jnp.logical_and(block == 1, item >= 1)))
         def _():
-            if item >= 2:
-                merge_cross(item - 2)
-            if item >= 3:
-                finish(item - 3)
-
-    @pl.when(is_cross)
-    def _():
-        merge_cross(3)
-        finish(2)
-        merge_cross(4)
-        finish(3)
-        finish(4)
+            merge_self(item - 1)
+
+    q_ready(0)
+    kv_ready(0)
+    stage(0, None, True)
+
+    def two_blocks(pair, carry):
+        step = 2 * pair
+        stage(step + 1, step, False)
+        after_block(step)
+
+        @pl.when(pair % 2 == 1)
+        def _():
+            q_ready((step + 2) // 4)
+            kv_ready((step + 2) // 4)
+
+        stage(step + 2, step + 1, True)
+        after_block(step + 1)
+        return carry
+
+    last = 4 * LOCAL_HEADS - 1
+    lax.fori_loop(0, (last - 1) // 2, two_blocks, 0)
+    stage(last, last - 1, False)
+    after_block(jnp.int32(last - 1))
+    stage(None, last, True)
+    on_self(lambda: merge_self(4))
+    on_self(self_mix)
+    send_fresh()
+    on_cross(
+        lambda: finish(1),
+        lambda: merge_cross(2),
+        lambda: merge_cross(3),
+        lambda: finish(2),
+        lambda: finish(3),
+        lambda: merge_cross(4),
+        lambda: finish(4),
+    )
 
     @pl.when(is_root)
     def _():
@@ -808,8 +873,9 @@
             for group in range(4):
                 att_result(item, group).wait_recv()
 
-    for copy in waits_at_end:
-        copy.wait_send()
+    for item in range(LOCAL_HEADS + 1):
+        for copy in kv_spread_copies(item) + kv_pushes(item):
+            copy.wait_send()
     for item in range(LOCAL_HEADS):
         for copy in piece_copies(item, 0):
             copy.wait_send()
@@ -885,6 +951,9 @@
             i32(8, 8, 128),
             bf16(LOCAL_HEADS, 1024, HDIM),
             f32(QBLOCK, KEYS),
+            f32(QBLOCK, KEYS),
+            f32(QBLOCK, 128),
+            f32(QBLOCK, 128),
             i32(1, KEYS),
             bf16(LOCAL_HEADS, 1024, HDIM),
             f32(LOCAL_HEADS, 2, 8, 128),

time: 94.5 us -> 84 us (0.89)
  the two profiles are of different devices: /device:TPU:56 before, /device:TPU:17 now
where the time goes in v4:
time: 84 us; the launch traced here: 83.5 us
  Pallas kernels  78.9 us (94%)
  local copies, waits for them, and re-layouts  3.32 us (4%)
  between operations  1.31 us (2%)
    pallas_call x1, Pallas kernels, span(): pl.pallas_call(span_kernel, out_shape=(jax.ShapeDtypeStruct((TOKENS, HD),...  78.9 us
    unnamed x7, local copies, waits for them, and re-layouts  3.32 us

profile of v4, /device:TPU:17, one launch (start us, length us, event | category | flops | bytes accessed | tf_op | source)
XLA Modules:
  0.0 83.5 jit_solution(5371462094199982566)
XLA Ops:
  1.3 78.9 %span.1 = (bf16[128,2560]{1,0:T(8,128)(2,1)}, f32[20,16,128]{2,1,0:T(8,128)}, bf16[8,5120]{1,0:T(8,128)(2,1)}) custom-call(bf16[128,2560]{1,0:T(8,128)(2,1)} %bitcast.11, f32[20,128,128]{2,1,0:T(8,128)} %bitcast.9, f32[16]{0:T(128)} %table_hbm.1, s32[1,20]{1,0:T(1,128)} %rate_hbm.1, f32[20,1,128]{2,1,0:T(1,128)} %bitcast.14, f32[1,2560]{1,0:T(1,128)} %query_gain_hbm.1, ...), custom_call_target="tpu_custom_call" | custom-call | tf_op jit(solution)/shard_map/span/pallas_call | solution.py:925
  80.1 0.0 copy-start
  80.2 0.0 copy-start.1
  80.2 2.0 %copy.19 = bf16[1,128,2560]{2,1,0:T(8,128)(2,1)} copy(bf16[1,128,2560]{2,1,0:T(8,128)(2,1)} %bitcast.10) | data formatting | bytes 1310720
  82.2 0.0 copy-done
  82.2 0.7 copy.20
  82.8 0.0 copy-done.1
  82.8 0.6 copy.21
Async XLA Ops:
  80.1 2.0 %copy-start = (f32[20,16,128]{2,1,0:T(8,128)S(1)}, f32[20,16,128]{2,1,0:T(8,128)}, u32[]{:S(2)}) copy-start(f32[20,16,128]{2,1,0:T(8,128)} %get-tuple-element.7) | copy-start | bytes 491524
  80.2 2.7 %copy-start.1 = (bf16[8,5120]{1,0:T(8,128)(2,1)S(1)}, bf16[8,5120]{1,0:T(8,128)(2,1)}, u32[]{:S(2)}) copy-start(bf16[8,5120]{1,0:T(8,128)(2,1)} %get-tuple-element.8) | copy-start | bytes 245764

commit v5 on v4

--- a/solution.py
+++ b/solution.py
@@ -484,8 +484,10 @@
     own_fresh = pltpu.make_async_copy(fresh_rows(section), fresh, s_local.at[4])
 
     def fresh_copy(by):
-        to = lax.rem(section + by, 16)
+        to = lax.rem(section + 2 * by, 16)
         return remote(fresh_rows(to), fresh, f_send.at[by], f_recv.at[0], (to, seq))
+
+    fresh_across = remote(fresh, fresh, f_send.at[0], f_recv.at[1], sibling)
 
     first_j = 1 - own_j
 
@@ -734,7 +736,7 @@
         @pl.when(is_root)
         def _():
             own_fresh.start()
-            for by in range(1, 16):
+            for by in range(1, 8):
                 fresh_copy(by).start()
 
     def own(item):
@@ -778,16 +780,16 @@
     place_setup()
 
     hooks = {
-        15: (keep_state,),
         0: (lambda: own(4), lambda: on_self(lambda: q_relay(2))),
         1: (lambda: kv_forward(3),),
         2: (lambda: kv_far(2),),
         3: (lambda: on_self(lambda: q_relay(3)),),
         4: (lambda: kv_forward(4),),
         5: (lambda: kv_far(3),),
-        7: (lambda: on_self(lambda: q_relay(4)),),
-        8: (lambda: kv_far(4), lambda: on_self(send_updates)),
+        6: (lambda: on_self(lambda: q_relay(4)),),
+        7: (lambda: kv_far(4), lambda: on_self(send_updates)),
         12: (lambda: on_cross(lambda: merge_cross(0)),),
+        14: (keep_state,),
         16: (lambda: on_cross(lambda: finish(0), lambda: merge_cross(1)),),
     }
 
@@ -850,9 +852,17 @@
     def _():
         own_fresh.wait()
 
-    @pl.when(jnp.logical_not(is_root))
+    @pl.when(jnp.logical_and(core == 1, jnp.logical_not(is_root)))
     def _():
         fresh_copy(1).wait_recv()
+
+    @pl.when(core == 1)
+    def _():
+        fresh_across.start()
+
+    @pl.when(core == 0)
+    def _():
+        fresh_across.wait_recv()
 
     both = fresh[...].astype(jnp.float32)
     new_rows = jnp.where(core == 0, both[0:8], both[8:16])
@@ -901,9 +911,13 @@
         for group in range(4):
             self_result(group).wait_send()
 
+    @pl.when(core == 1)
+    def _():
+        fresh_across.wait_send()
+
     @pl.when(is_root)
     def _():
-        for by in range(1, 16):
+        for by in range(1, 8):
             fresh_copy(by).wait_send()
 
 
@@ -999,8 +1013,8 @@
             dma((LOCAL_HEADS, 4)),
             dma((4,)),
             dma((4,)),
-            dma((16,)),
-            dma((1,)),
+            dma((8,)),
+            dma((2,)),
         ],
         compiler_params=pltpu.CompilerParams(
             collective_id=0, has_side_effects=True, vmem_limit_bytes=58 * 1024 * 1024

time: 84 us -> 82.2 us (0.979)
  Pallas kernels: 78.9 us -> 77.5 us
    pallas_call x1, Pallas kernels: 78.9 us -> 77.5 us  [span(): pl.pallas_call(span_kernel, out_shape=(jax.ShapeDtypeStruct((TOKENS, HD),...]
where the time goes in v5:
time: 82.2 us; the launch traced here: 82.1 us
  Pallas kernels  77.5 us (94%)
  local copies, waits for them, and re-layouts  3.32 us (4%)
  between operations  1.31 us (2%)
    pallas_call x1, Pallas kernels, span(): pl.pallas_call(span_kernel, out_shape=(jax.ShapeDtypeStruct((TOKENS, HD),...  77.5 us
    unnamed x7, local copies, waits for them, and re-layouts  3.32 us

profile of v5, /device:TPU:17, one launch (start us, length us, event | category | flops | bytes accessed | tf_op | source)
XLA Modules:
  0.0 82.1 jit_solution(14900457145567927453)
XLA Ops:
  1.3 77.5 %span.1 = (bf16[128,2560]{1,0:T(8,128)(2,1)}, f32[20,16,128]{2,1,0:T(8,128)}, bf16[8,5120]{1,0:T(8,128)(2,1)}) custom-call(bf16[128,2560]{1,0:T(8,128)(2,1)} %bitcast.11, f32[20,128,128]{2,1,0:T(8,128)} %bitcast.9, f32[16]{0:T(128)} %table_hbm.1, s32[1,20]{1,0:T(1,128)} %rate_hbm.1, f32[20,1,128]{2,1,0:T(1,128)} %bitcast.14, f32[1,2560]{1,0:T(1,128)} %query_gain_hbm.1, ...), custom_call_target="tpu_custom_call" | custom-call | tf_op jit(solution)/shard_map/span/pallas_call | solution.py:939
  78.8 0.0 copy-start
  78.8 0.0 copy-start.1
  78.8 2.0 %copy.19 = bf16[1,128,2560]{2,1,0:T(8,128)(2,1)} copy(bf16[1,128,2560]{2,1,0:T(8,128)(2,1)} %bitcast.10) | data formatting | bytes 1310720
  80.8 0.0 copy-done
  80.8 0.7 copy.20
  81.5 0.0 copy-done.1
  81.5 0.6 copy.21
Async XLA Ops:
  78.8 2.0 %copy-start = (f32[20,16,128]{2,1,0:T(8,128)S(1)}, f32[20,16,128]{2,1,0:T(8,128)}, u32[]{:S(2)}) copy-start(f32[20,16,128]{2,1,0:T(8,128)} %get-tuple-element.7) | copy-start | bytes 491524
  78.8 2.7 %copy-start.1 = (bf16[8,5120]{1,0:T(8,128)(2,1)S(1)}, bf16[8,5120]{1,0:T(8,128)(2,1)}, u32[]{:S(2)}) copy-start(bf16[8,5120]{1,0:T(8,128)(2,1)} %get-tuple-element.8) | copy-start | bytes 245764

commit v6 on v5

--- a/solution.py
+++ b/solution.py
@@ -455,7 +455,7 @@
             state_out[pl.ds(head, 1)] = now[None]
             return carry
 
-        lax.fori_loop(0, HEADS, one, 0)
+        lax.fori_loop(0, HEADS, one, 0, unroll=4)
 
     def mix(first, last):
         def one(head, carry):

time: 82.2 us -> 82 us (level)
  no operation moved by 1% of the time
where the time goes in v6:
time: 82 us; the launch traced here: 81.9 us
  Pallas kernels  77.3 us (94%)
  local copies, waits for them, and re-layouts  3.32 us (4%)
  between operations  1.31 us (2%)
    pallas_call x1, Pallas kernels, span(): pl.pallas_call(span_kernel, out_shape=(jax.ShapeDtypeStruct((TOKENS, HD),...  77.3 us
    unnamed x7, local copies, waits for them, and re-layouts  3.32 us

profile of v6, /device:TPU:17, one launch (start us, length us, event | category | flops | bytes accessed | tf_op | source)
XLA Modules:
  0.0 81.9 jit_solution(10618462866789163012)
XLA Ops:
  1.3 77.3 %span.1 = (bf16[128,2560]{1,0:T(8,128)(2,1)}, f32[20,16,128]{2,1,0:T(8,128)}, bf16[8,5120]{1,0:T(8,128)(2,1)}) custom-call(bf16[128,2560]{1,0:T(8,128)(2,1)} %bitcast.11, f32[20,128,128]{2,1,0:T(8,128)} %bitcast.9, f32[16]{0:T(128)} %table_hbm.1, s32[1,20]{1,0:T(1,128)} %rate_hbm.1, f32[20,1,128]{2,1,0:T(1,128)} %bitcast.14, f32[1,2560]{1,0:T(1,128)} %query_gain_hbm.1, ...), custom_call_target="tpu_custom_call" | custom-call | tf_op jit(solution)/shard_map/span/pallas_call | solution.py:939
  78.6 0.0 copy-start
  78.6 0.0 copy-start.1
  78.6 2.0 %copy.19 = bf16[1,128,2560]{2,1,0:T(8,128)(2,1)} copy(bf16[1,128,2560]{2,1,0:T(8,128)(2,1)} %bitcast.10) | data formatting | bytes 1310720
  80.6 0.0 copy-done
  80.6 0.7 copy.20
  81.3 0.0 copy-done.1
  81.3 0.6 copy.21
Async XLA Ops:
  78.6 2.0 %copy-start = (f32[20,16,128]{2,1,0:T(8,128)S(1)}, f32[20,16,128]{2,1,0:T(8,128)}, u32[]{:S(2)}) copy-start(f32[20,16,128]{2,1,0:T(8,128)} %get-tuple-element.7) | copy-start | bytes 491524
  78.6 2.7 %copy-start.1 = (bf16[8,5120]{1,0:T(8,128)(2,1)S(1)}, bf16[8,5120]{1,0:T(8,128)(2,1)}, u32[]{:S(2)}) copy-start(bf16[8,5120]{1,0:T(8,128)(2,1)} %get-tuple-element.8) | copy-start | bytes 245764
